TPU v7x, 32 devices: a whole 2x2x4 slice. The times are simulated.
32 devices in a mesh: blk: 16 (over z, x, core), col: 2 (over y).
Axes of the slice: x: 2, y: 2, z: 4, core: 2. Of those that a mesh axis runs over, the one named last changes fastest.
Arguments:
- tiles: bfloat16 [384, 128, 128], P('blk'), may hold values from -0.21875 to 0.21875
- tile_rows: int32 [384], P('blk'), may hold values from 0 to 3, as said below
- tile_cols: int32 [384], P('blk'), may hold values from 0 to 511, as said below
- tile_count: int32 [16], P('blk'), may hold values from 3 to 24, as said below
- sketch: bfloat16 [65536, 512], P('blk', 'col'), may hold values from -6 to 6
- variant_scale: bfloat16 [65536], P('blk'), may hold values from 0.5 to 2
Outputs:
- basis_rows: float32 [8192, 512], P('blk', 'col')
Inputs may be any that keep to these rules, and one draw needn't show every extreme that they name: `tile_count`: each row group has 24, 12, 6 or 3 live slots, and at least one group has all 24 live. `tile_rows`: no two slots of a row group name the same block row and block column. Slots at or past their group's count are not part of the matrix. `tile_cols`: within one row group, all slots whose block columns lie in the same run of 32 block columns that starts at a multiple of 32 name the same block column.
All inputs are finite; a program needn't handle non-finite values.
Results may differ from a plain program's by a relative error of at most 0.0059.
Values may be sent and summed in bfloat16 or wider, within the bound.
A program may use at most 128 MiB of HBM per device.

v0:
```python
import jax
import jax.numpy as jnp
from jax import lax
from jax.sharding import PartitionSpec as P

TPR = 6
RB_DEV = 4


def from_partner(x, axis, apart):
    return lax.ppermute(x, axis, [(i, i ^ 1 << apart) for i in range(lax.axis_size(axis))])


def invert_factor(gram_matrix):
    lower_factor = jnp.linalg.cholesky(gram_matrix)
    identity = jnp.eye(gram_matrix.shape[0], dtype=jnp.float32)
    return jax.scipy.linalg.solve_triangular(lower_factor, identity, lower=True)


def gram_of(row_block):
    return lax.dot_general(
        row_block, row_block, (((0,), (0,)), ((), ())), preferred_element_type=jnp.float32
    )


def local(tiles, tile_rows, tile_cols, tile_count, sketch, variant_scale):
    sketch_width = sketch.shape[1]
    tile_edge = tiles.shape[1]
    owners = lax.axis_size("blk")
    own_blocks = sketch.shape[0] // tile_edge
    group_size = tiles.shape[0] // TPR
    own_rows = RB_DEV
    live_count = tile_count[0]
    turn_count = (live_count + group_size - 1) // group_size
    slot_ids = jnp.arange(group_size, dtype=jnp.int32)
    every_slot = jnp.arange(tiles.shape[0], dtype=jnp.int32)
    owner_ids = jnp.arange(owners, dtype=jnp.int32)
    block_ids = jnp.arange(own_blocks, dtype=jnp.int32)
    slot_owner = tile_cols // own_blocks
    slot_hits = (slot_owner[None, :] == owner_ids[:, None]) & (every_slot < live_count)[None, :]
    wanted = jnp.max(jnp.where(slot_hits, (tile_cols % own_blocks)[None, :], 0), axis=1)
    asked_blocks = lax.all_to_all(
        wanted.reshape(owners, 1), "blk", split_axis=0, concat_axis=0, tiled=True
    ).reshape(owners)

    def serve_blocks(own_panel):
        return jnp.take(
            own_panel.reshape(own_blocks, tile_edge, own_panel.shape[1]), asked_blocks, axis=0
        )

    own_scale = variant_scale.astype(jnp.float32)
    scaled_own = (own_scale[:, None] * sketch.astype(jnp.float32)).astype(jnp.bfloat16)
    fetched_sketch = lax.all_to_all(
        serve_blocks(scaled_own), "blk", split_axis=0, concat_axis=0, tiled=True
    )

    def take_group(turn_index):
        first_slot = turn_index * group_size
        tile_group = lax.dynamic_slice_in_dim(tiles, first_slot, group_size, 0)
        row_group = lax.dynamic_slice_in_dim(tile_rows, first_slot, group_size, 0)
        col_group = lax.dynamic_slice_in_dim(tile_cols, first_slot, group_size, 0)
        live_mask = (first_slot + slot_ids < live_count).astype(jnp.float32)
        return (tile_group, row_group, col_group, live_mask)

    def forward(fetched):

        def forward_step(turn_index, accumulated):
            tile_group, row_group, col_group, live_mask = take_group(turn_index)
            selected = jnp.take(fetched, col_group // own_blocks, axis=0)
            products = jnp.einsum(
                "tij,tjk->tik", tile_group, selected, preferred_element_type=jnp.float32
            )
            return accumulated.at[row_group].add(products * live_mask[:, None, None])

        start_rows = jnp.zeros((own_rows, tile_edge, sketch_width), jnp.float32)
        accumulated = lax.fori_loop(0, turn_count, forward_step, start_rows)
        return accumulated.reshape(own_rows * tile_edge, sketch_width)

    range_rows = forward(fetched_sketch).astype(jnp.bfloat16)
    row_blocks = range_rows.reshape(own_rows, tile_edge, sketch_width)

    def back_step(turn_index, accumulated):
        tile_group, row_group, col_group, live_mask = take_group(turn_index)
        selected = jnp.take(row_blocks, row_group, axis=0)
        products = jnp.einsum(
            "tji,tjk->tik", tile_group, selected, preferred_element_type=jnp.float32
        )
        return accumulated.at[col_group // own_blocks].add(products * live_mask[:, None, None])

    start_back = jnp.zeros((owners, tile_edge, sketch_width), jnp.float32)
    group_terms = lax.fori_loop(0, turn_count, back_step, start_back).astype(jnp.bfloat16)
    block_select = (asked_blocks[:, None] == block_ids[None, :]).astype(jnp.bfloat16)
    arrived_terms = lax.all_to_all(group_terms, "blk", split_axis=0, concat_axis=0, tiled=True)
    own_back = jnp.einsum(
        "qb,qik->bik", block_select, arrived_terms, preferred_element_type=jnp.float32
    )
    own_back = own_back.reshape(own_blocks * tile_edge, arrived_terms.shape[2])
    weighted_own = ((own_scale * own_scale)[:, None] * own_back).astype(jnp.bfloat16)
    fetched_weighted = lax.all_to_all(
        serve_blocks(weighted_own), "blk", split_axis=0, concat_axis=0, tiled=True
    )
    power_rows = forward(fetched_weighted).astype(jnp.bfloat16)
    total_rows = own_rows * tile_edge * lax.axis_size("blk")
    partner_half = from_partner(power_rows, "col", 0)
    col_index = lax.axis_index("col")
    all_columns = jnp.where(
        col_index == 0,
        jnp.concatenate([power_rows, partner_half], axis=1),
        jnp.concatenate([partner_half, power_rows], axis=1),
    )
    gram_matrix = lax.psum(gram_of(all_columns), "blk") / total_rows
    inverse = invert_factor(gram_matrix)
    inverse_rows = lax.dynamic_slice_in_dim(inverse, col_index * sketch_width, sketch_width, 0)
    basis_rows = jnp.dot(
        all_columns.astype(jnp.float32), inverse_rows.T, precision=lax.Precision.HIGHEST
    )
    return basis_rows


def solution(mesh):
    placed = (P("blk", None, None), P("blk"), P("blk"), P("blk"), P("blk", "col"), P("blk"))
    return jax.shard_map(
        local, mesh=mesh, in_specs=placed, out_specs=P("blk", "col"), check_vma=False
    )
```

profile of v0, /device:TPU:0, one launch (start us, length us, event | category | flops | bytes accessed | tf_op | source)
XLA Modules:
  0.0 440.9 jit_solution(12274809044485994009)
XLA Ops:
  8.7 7.4 %all-to-all-start = ((s32[16,1,1]{2,1,0:T(1,128)}), s32[16,1,1]{2,1,0:T(1,128)S(1)}, u32[]{:S(2)}, u32[]{:S(2)}) async-start(s32[16,1,1]{2,1,0:T(1,128)} %copy.32), calls=%async_computation | async-start | bytes 16384 | tf_op jit(solution)/shard_map/all_to_all | solution.py:42
  16.7 1.9 multiply_convert_fusion.1
  18.7 3.7 all-to-all-done
  23.4 1.2 broadcast_select_fusion
  24.6 3.7 all-to-all-start.1
  28.3 22.9 %all-to-all-done.1 = bf16[16,128,256]{2,1,0:T(8,128)(2,1)S(1)} async-done(((bf16[16,128,256]{2,1,0:T(8,128)(2,1)}), bf16[16,128,256]{2,1,0:T(8,128)(2,1)S(1)}, u32[]{:S(2)}, u32[]{:S(2)}) %all-to-all-start.1) | async-done | bytes 1048608 | tf_op jit(solution)/shard_map/all_to_all | solution.py:53
  51.2 10.6 %while.41 = (s32[]{:T(128)}, f32[4,128,256]{2,1,0:T(8,128)S(1)}, s32[]{:T(128)}, s32[24]{0:T(128)S(1)}, bf16[24,128,128]{2,1,0:T(8,128)(2,1)}, /*index=5*/s32[24...) while((s32[]{:T(128)}, f32[4,128,256]{2,1,0:T(8,128)S(1)}, ...), condition=%wide.region_3.6_spmd.clone, body=%wide.region_1.5_spmd.clone.sunk | while | flops 33948784 | bytes 3019087 | solution.py:76
  52.5 1.2 convolution_multiply_fusion.6
  56.1 1.2 convolution_multiply_fusion.6
  59.6 1.2 convolution_multiply_fusion.6
  62.0 10.5 %while.42 = (s32[]{:T(128)}, f32[16,128,256]{2,1,0:T(8,128)S(1)}, s32[]{:T(128)}, s32[24]{0:T(128)S(1)}, bf16[24,128,128]{2,1,0:T(8,128)(2,1)}, /*index=5*/s32[2...) while((s32[]{:T(128)}, f32[16,128,256]{2,1,0:T(8,128)S(1)}, ...), condition=%wide.region_6.9_spmd.clone, body=%wide.region_4.8_spmd.clone.sunk | while | flops 33948784 | bytes 3019087 | solution.py:91
  63.3 1.2 convolution_multiply_fusion.7
  66.8 1.2 convolution_multiply_fusion.7
  70.4 1.2 convolution_multiply_fusion.7
  73.7 27.9 %all-to-all-start.2 = ((bf16[16,128,256]{2,1,0:T(8,128)(2,1)}), bf16[16,128,256]{2,1,0:T(8,128)(2,1)S(1)}, u32[]{:S(2)}, u32[]{:S(2)}) async-start(bf16[16,128,256]{2,1,0:T(8,128)(2,1)} %convert_element_type.69), calls=%async_computation.2 | async-start | bytes 2097152 | tf_op jit(solution)/shard_map/all_to_all | solution.py:93
  101.7 22.8 %all-to-all-done.2 = bf16[16,128,256]{2,1,0:T(8,128)(2,1)S(1)} async-done(((bf16[16,128,256]{2,1,0:T(8,128)(2,1)}), bf16[16,128,256]{2,1,0:T(8,128)(2,1)S(1)}, u32[]{:S(2)}, u32[]{:S(2)}) %all-to-all-start.2) | async-done | bytes 1048608 | tf_op jit(solution)/shard_map/all_to_all | solution.py:93
  124.5 1.8 multiply_convert_fusion
  126.3 1.2 copy.36
  128.1 1.2 broadcast_select_fusion.1
  129.3 6.9 %all-to-all-start.3 = ((bf16[16,128,256]{2,1,0:T(8,128)(2,1)}), bf16[16,128,256]{2,1,0:T(8,128)(2,1)S(1)}, u32[]{:S(2)}, u32[]{:S(2)}) async-start(bf16[16,128,256]{2,1,0:T(8,128)(2,1)} %broadcast_select_fusion.1), calls=%async_computation.3 | async-start | bytes 2097152 | tf_op jit(solution)/shard_map/all_to_all | solution.py:99
  136.2 22.9 %all-to-all-done.3 = bf16[16,128,256]{2,1,0:T(8,128)(2,1)S(1)} async-done(((bf16[16,128,256]{2,1,0:T(8,128)(2,1)}), bf16[16,128,256]{2,1,0:T(8,128)(2,1)S(1)}, u32[]{:S(2)}, u32[]{:S(2)}) %all-to-all-start.3) | async-done | bytes 1048608 | tf_op jit(solution)/shard_map/all_to_all | solution.py:99
  159.1 10.7 %while.43 = (s32[]{:T(128)}, f32[4,128,256]{2,1,0:T(8,128)S(1)}, s32[]{:T(128)}, s32[24]{0:T(128)S(1)}, bf16[24,128,128]{2,1,0:T(8,128)(2,1)}, /*index=5*/s32[24...) while((s32[]{:T(128)}, f32[4,128,256]{2,1,0:T(8,128)S(1)}, ...), condition=%wide.region_9.12_spmd.clone, body=%wide.region_7.11_spmd.clone.sunk | while | flops 33948784 | bytes 3019087 | solution.py:76
  160.5 1.2 convolution_multiply_fusion.8
  164.0 1.2 convolution_multiply_fusion.8
  167.5 1.2 convolution_multiply_fusion.8
  169.9 1.6 collective-permute-start
  171.5 4.9 %collective-permute-done = bf16[512,256]{1,0:T(8,128)(2,1)S(1)} collective-permute-done((bf16[512,256]{1,0:T(8,128)(2,1)S(1)}, bf16[512,256]{1,0:T(8,128)(2,1)S(1)}, u32[]{:S(2)}, u32[]{:S(2)}) %collective-permute-start) | collective-permute-done | bytes 262176 | tf_op jit(solution)/shard_map/ppermute | solution.py:11
  176.3 1.5 fusion.50
  179.1 106.0 %all-reduce.3.cloned.1.call-done = f32[512,512]{0,1:T(8,128)} async-done(((f32[512,512]{0,1:T(8,128)}), f32[512,512]{0,1:T(8,128)}) %all-reduce.3.cloned.1.call-update) | async-done | bytes 1048592 | tf_op jit(solution)/shard_map/psum | solution.py:111
  285.1 1.4 broadcast_multiply_fusion
  287.1 11.7 %cholesky.104 = f32[128,128]{1,0:T(8,128)S(1)} custom-call(f32[128,128]{1,0:T(8,128)S(1)} %cholesky.266), custom_call_target="Cholesky" | custom-call | tf_op jit(solution)/shard_map/jit(cholesky)/cholesky | solution.py:15
  299.0 9.8 %custom-call.31 = f32[1,128,128]{1,2,0:T(8,128)S(1)} custom-call(f32[1,128,128]{2,1,0:T(8,128)S(1)} %get-tuple-element.550), custom_call_target="InvertDiagBlocksLowerTriangular" | custom-call | tf_op jit(solution)/shard_map/jit(cholesky)/cholesky | solution.py:15
  309.5 11.7 %cholesky.217 = f32[128,128]{1,0:T(8,128)S(1)} custom-call(f32[128,128]{1,0:T(8,128)S(1)} %cholesky.270), custom_call_target="Cholesky" | custom-call | tf_op jit(solution)/shard_map/jit(cholesky)/cholesky | solution.py:15
  321.2 10.0 %custom-call.32 = f32[1,128,128]{1,2,0:T(8,128)S(1)} custom-call(f32[1,128,128]{2,1,0:T(8,128)S(1)} %get-tuple-element.547), custom_call_target="InvertDiagBlocksLowerTriangular" | custom-call | tf_op jit(solution)/shard_map/jit(cholesky)/cholesky | solution.py:15
  331.9 12.3 %cholesky.238 = f32[128,128]{1,0:T(8,128)} custom-call(f32[128,128]{1,0:T(8,128)S(1)} %cholesky.275), custom_call_target="Cholesky" | custom-call | tf_op jit(solution)/shard_map/jit(cholesky)/cholesky | solution.py:15
  344.2 1.6 select_reduce_fusion.1
  346.5 11.3 %custom-call.33 = f32[1,128,128]{1,2,0:T(8,128)} custom-call(f32[1,128,128]{2,1,0:T(8,128)} %get-tuple-element.544), custom_call_target="InvertDiagBlocksLowerTriangular" | custom-call | tf_op jit(solution)/shard_map/jit(cholesky)/cholesky | solution.py:15
  359.2 11.9 %cholesky.255 = f32[128,128]{1,0:T(8,128)S(1)} custom-call(f32[128,128]{1,0:T(8,128)S(1)} %convolution_subtract_fusion.5), custom_call_target="Cholesky" | custom-call | tf_op jit(solution)/shard_map/jit(cholesky)/cholesky | solution.py:15
  375.2 10.6 %while.40 = (s32[]{:T(128)}, f32[512,512]{1,0:T(8,128)S(1)}, s32[4,2]{0,1:T(2,128)S(1)}, f32[4,128,128]{2,1,0:T(8,128)}, s32[]{:T(128)}) while((s32[]{:T(128)}, f32[512,512]{1,0:T(8,128)S(1)}, s32[4,2]{0,1:T(2,128)S(1)}, f32[4,128,128]{2,1,0:T(8,128)}, s32[]{:T(128)}) %tuple.129), condition=%wide.while_cond, body=%wide.while_body.sunk | while | flops 2 | bytes 132705 | solution.py:17
  375.9 2.0 bitcast_dynamic-update-slice_fusion.2
  378.6 2.0 bitcast_dynamic-update-slice_fusion.2
  381.2 2.0 bitcast_dynamic-update-slice_fusion.2
  383.8 2.0 bitcast_dynamic-update-slice_fusion.2
  385.8 40.1 %custom-call.34 = f32[4,128,128]{1,2,0:T(8,128)S(1)} custom-call(f32[4,128,128]{2,1,0:T(8,128)} %get-tuple-element.368), custom_call_target="InvertDiagBlocksLowerTriangular" | custom-call | tf_op jit(solution)/shard_map/jit(_solve_triangular)/triangular_solve | solution.py:17
  427.0 1.3 fusion.54
  428.8 1.3 fusion.52
  430.7 1.3 fusion.51
  432.0 1.6 fusion.34
  (122 shorter events, 37.5 us)
Async XLA Ops:
  8.7 13.7 %all-to-all-start = ((s32[16,1,1]{2,1,0:T(1,128)}), s32[16,1,1]{2,1,0:T(1,128)S(1)}, u32[]{:S(2)}, u32[]{:S(2)}) async-start(s32[16,1,1]{2,1,0:T(1,128)} %copy.32), calls=%async_computation | async-start | bytes 16384 | tf_op jit(solution)/shard_map/all_to_all | solution.py:42
  23.4 27.8 %copy-start.5 = (s32[24]{0:T(128)S(1)}, s32[24]{0:T(128)}, u32[]{:S(2)}) copy-start(s32[24]{0:T(128)} %param.18) | copy-start | bytes 292
  23.4 27.8 %copy-start.7 = (s32[24]{0:T(128)S(1)}, s32[24]{0:T(128)}, u32[]{:S(2)}) copy-start(s32[24]{0:T(128)} %param.17) | copy-start | bytes 292
  24.6 26.6 %all-to-all-start.1 = ((bf16[16,128,256]{2,1,0:T(8,128)(2,1)}), bf16[16,128,256]{2,1,0:T(8,128)(2,1)S(1)}, u32[]{:S(2)}, u32[]{:S(2)}) async-start(bf16[16,128,256]{2,1,0:T(8,128)(2,1)} %broadcast_select_fusion), calls=%async_computation.1 | async-start | bytes 2097152 | tf_op jit(solution)/shard_map/all_to_all | solution.py:53
  72.5 29.1 %copy-start.6 = (bf16[4096]{0:T(1024)(128)(2,1)S(1)}, bf16[4096]{0:T(1024)(128)(2,1)}, u32[]{:S(2)}) copy-start(bf16[4096]{0:T(1024)(128)(2,1)} %param.21) | copy-start | bytes 24580
  73.7 50.9 %all-to-all-start.2 = ((bf16[16,128,256]{2,1,0:T(8,128)(2,1)}), bf16[16,128,256]{2,1,0:T(8,128)(2,1)S(1)}, u32[]{:S(2)}, u32[]{:S(2)}) async-start(bf16[16,128,256]{2,1,0:T(8,128)(2,1)} %convert_element_type.69), calls=%async_computation.2 | async-start | bytes 2097152 | tf_op jit(solution)/shard_map/all_to_all | solution.py:93
  129.3 29.8 %all-to-all-start.3 = ((bf16[16,128,256]{2,1,0:T(8,128)(2,1)}), bf16[16,128,256]{2,1,0:T(8,128)(2,1)S(1)}, u32[]{:S(2)}, u32[]{:S(2)}) async-start(bf16[16,128,256]{2,1,0:T(8,128)(2,1)} %broadcast_select_fusion.1), calls=%async_computation.3 | async-start | bytes 2097152 | tf_op jit(solution)/shard_map/all_to_all | solution.py:99
  136.1 149.0 %all-reduce.3.cloned.1.call-start = ((), (), s32[]{:S(2)}) async-start(), calls=%async_computation.4 | async-start | bytes 2097152 | tf_op jit(solution)/shard_map/psum | solution.py:111
  169.9 8.1 %copy-start.2 = (bf16[4,128,256]{2,1,0:T(8,128)(2,1)}, bf16[4,128,256]{2,1,0:T(8,128)(2,1)S(1)}, u32[]{:S(2)}) copy-start(bf16[4,128,256]{2,1,0:T(8,128)(2,1)S(1)} %convert_element_type.71) | copy-start | bytes 786436
  169.9 6.4 %collective-permute-start = (bf16[512,256]{1,0:T(8,128)(2,1)S(1)}, bf16[512,256]{1,0:T(8,128)(2,1)S(1)}, u32[]{:S(2)}, u32[]{:S(2)}) collective-permute-start(bf16[512,256]{1,0:T(8,128)(2,1)S(1)} %bitcast.60), channel_id=1, source_target_pairs={{0,1},{1,0},{2,3},{3,2},{4,5},{5,4},{6,7},{7,6},{8,9},{9,8},{10,11... | collective-permute-start | bytes 786440 | tf_op jit(solution)/shard_map/ppermute | solution.py:11
  176.3 1.5 copy-start.8
  285.1 1.8 copy-start
  344.2 82.4 %copy-start.1 = (f32[512,512]{1,0:T(8,128)S(1)}, f32[512,512]{1,0:T(8,128)}, u32[]{:S(2)}) copy-start(f32[512,512]{1,0:T(8,128)} %fusion.39) | copy-start | bytes 3145732
  425.9 0.7 copy-start.4
  427.0 5.0 %copy-start.3 = (bf16[4,128,256]{2,1,0:T(8,128)(2,1)S(1)}, bf16[4,128,256]{2,1,0:T(8,128)(2,1)}, u32[]{:S(2)}) copy-start(bf16[4,128,256]{2,1,0:T(8,128)(2,1)} %copy-done.2) | copy-start | bytes 786436
  427.0 5.0 %copy-start.9 = (bf16[512,256]{1,0:T(8,128)(2,1)S(1)}, bf16[512,256]{1,0:T(8,128)(2,1)}, u32[]{:S(2)}) copy-start(bf16[512,256]{1,0:T(8,128)(2,1)} %copy-done.8) | copy-start | bytes 786436
Sparse Core Ops, SparseCore 0:
  178.0 107.0 all-reduce.2
where the time goes:
time: 447 us; the launch traced here: 441 us
  waiting for transfers between devices  183 us (41%)
  other arithmetic  148 us (33%)
  starting transfers between devices  47.4 us (11%)
  matrix products  23.9 us (5%)
  local copies, waits for them, and re-layouts  20 us (4%)
  between operations  17.5 us (4%)
    psum x1, waiting for transfers between devices, local(): gram_matrix = lax.psum(gram_of(all_columns), 'blk') / total_rows  106 us
    another operation x14, other arithmetic, invert_factor(): lower_factor = jnp.linalg.cholesky(gram_matrix)  82.5 us
    another operation x3, other arithmetic, invert_factor(): return jax.scipy.linalg.solve_triangular(lower_factor, identity, lower=True)  40.3 us
    all_to_all x1, starting transfers between devices, local(): lax.all_to_all(group_terms, 'blk', split_axis=0, concat_axis=0, tiled=True)  27.9 us
    all_to_all x1, waiting for transfers between devices, local(): lax.all_to_all(serve_blocks(weighted_own), 'blk', split_axis=0, concat_ax...  22.9 us
    all_to_all x1, waiting for transfers between devices, local(): lax.all_to_all(serve_blocks(scaled_own), 'blk', split_axis=0, concat_axis...  22.9 us
    all_to_all x1, waiting for transfers between devices, local(): lax.all_to_all(group_terms, 'blk', split_axis=0, concat_axis=0, tiled=True)  22.8 us
    another operation x14, local copies, waits for them, and re-layouts  10.6 us
  transfers between devices with their start and end apart: 6, of which 6 were waited for; matrix products, arithmetic and copies ran while one was open for 1% of the time, Pallas kernels for 0%

commit v1 on v0

v1 whole, which is shorter than its diff:
```python
import functools
import jax
import jax.numpy as jnp
from jax import lax
from jax.experimental import pallas as pl
from jax.experimental.pallas import tpu as pltpu
from jax.sharding import PartitionSpec as P

TPR = 6
RB_DEV = 4
STEP = 3
PANEL = 8
VMEM_BYTES = 60 * 2**20
HIGHEST = lax.Precision.HIGHEST

SMEM_SPEC = pl.BlockSpec(memory_space=pltpu.SMEM)
VMEM_SPEC = pl.BlockSpec(memory_space=pltpu.VMEM)
PARAMS = pltpu.CompilerParams(vmem_limit_bytes=VMEM_BYTES)


def forward_rows(rows_ref, owner_ref, count, tiles_ref, fetched_ref, acc_ref):
    acc_ref[...] = jnp.zeros_like(acc_ref)

    def turn(index, carry):
        slots = [index * STEP + step for step in range(STEP)]
        products = [
            jnp.dot(
                tiles_ref[slot], fetched_ref[owner_ref[slot]], preferred_element_type=jnp.float32
            )
            for slot in slots
        ]
        for slot, product in zip(slots, products):
            acc_ref[rows_ref[slot]] += product
        return carry

    lax.fori_loop(0, count // STEP, turn, 0)


def range_kernel(rows_ref, owner_ref, count_ref, tiles_ref, fetched_ref, terms_ref, acc_ref, held_ref, sum_ref):
    count = count_ref[0]
    forward_rows(rows_ref, owner_ref, count, tiles_ref, fetched_ref, acc_ref)
    held_ref[...] = acc_ref[...].astype(jnp.bfloat16)
    sum_ref[...] = jnp.zeros_like(sum_ref)

    def turn(index, carry):
        slots = [index * STEP + step for step in range(STEP)]
        products = [
            lax.dot_general(
                tiles_ref[slot],
                held_ref[rows_ref[slot]],
                (((0,), (0,)), ((), ())),
                preferred_element_type=jnp.float32,
            )
            for slot in slots
        ]
        for slot, product in zip(slots, products):
            sum_ref[owner_ref[slot]] += product
        return carry

    lax.fori_loop(0, count // STEP, turn, 0)
    terms_ref[...] = sum_ref[...].astype(jnp.bfloat16)


def power_kernel(rows_ref, owner_ref, count_ref, tiles_ref, fetched_ref, out_ref, acc_ref):
    forward_rows(rows_ref, owner_ref, count_ref[0], tiles_ref, fetched_ref, acc_ref)
    out_ref[...] = acc_ref[...].astype(jnp.bfloat16)


def weight_kernel(asked_ref, square_ref, terms_ref, out_ref, sum_ref):
    owners, edge, width = terms_ref.shape

    def clear(q, carry):
        sum_ref[asked_ref[q]] = jnp.zeros((edge, width), jnp.float32)
        return carry

    def gather(q, carry):
        sum_ref[asked_ref[q]] += terms_ref[q].astype(jnp.float32)
        return carry

    def scale(q, carry):
        total = sum_ref[asked_ref[q]]
        for part in range(0, width, edge):
            out_ref[q, :, part : part + edge] = (
                square_ref[q] * total[:, part : part + edge]
            ).astype(jnp.bfloat16)
        return carry

    lax.fori_loop(0, owners, clear, 0)
    lax.fori_loop(0, owners, gather, 0)
    lax.fori_loop(0, owners, scale, 0)


def invert_block(block):
    edge = block.shape[0]
    lanes = lax.broadcasted_iota(jnp.int32, (PANEL, edge), 1)
    sublanes = lax.broadcasted_iota(jnp.int32, (PANEL, edge), 0)
    strips = [block[start : start + PANEL, :] for start in range(0, edge, PANEL)]
    done = []
    for panel in range(len(strips)):
        first = panel * PANEL
        live = strips[panel:]
        columns = [
            [
                jnp.broadcast_to(strip[:, first + k : first + k + 1], (PANEL, edge))
                for strip in live
            ]
            for k in range(PANEL)
        ]
        inside = (lanes >= first) & (lanes < first + PANEL)
        unit = (lanes == first + sublanes).astype(jnp.float32)
        live = [
            jnp.where(inside, unit if at == 0 else 0.0, strip) for at, strip in enumerate(live)
        ]
        pivots = jnp.ones((PANEL, edge), jnp.float32)
        for i in range(PANEL):
            pivot = jnp.broadcast_to(columns[i][0][i : i + 1, :], (PANEL, edge))
            pivots = jnp.where(sublanes == i, pivot, pivots)
            factor = 1.0 / pivot
            row = jnp.broadcast_to(live[0][i : i + 1, :], (PANEL, edge))
            heads = [
                jnp.broadcast_to(columns[k][0][i : i + 1, :], (PANEL, edge))
                for k in range(i + 1, PANEL)
            ]
            for at in range(len(live)):
                times = columns[i][at] * factor
                if at == 0:
                    times = jnp.where(sublanes > i, times, 0.0)
                live[at] = live[at] - times * row
                for k in range(i + 1, PANEL):
                    columns[k][at] = columns[k][at] - times * heads[k - i - 1]
        done.append(jnp.where(lanes <= first + sublanes, live[0] * lax.rsqrt(pivots), 0.0))
        strips = strips[: panel + 1] + live[1:]
    return jnp.concatenate(done, axis=0)


def basis_kernel(col_ref, gram_ref, rows_ref, out_ref, held_ref):
    size = gram_ref.shape[0]
    width = out_ref.shape[1]
    edge = 128
    held_ref[...] = gram_ref[...]
    for start in range(0, size, edge):
        stop = start + edge
        inverse = invert_block(held_ref[start:stop, start:stop])
        if start:
            before = jnp.dot(
                inverse, held_ref[start:stop, :start],
                precision=HIGHEST, preferred_element_type=jnp.float32,
            )
            held_ref[start:stop, :start] = before
        held_ref[start:stop, start:stop] = inverse
        if stop < size:
            panel = lax.dot_general(
                held_ref[stop:, start:stop], inverse, (((1,), (1,)), ((), ())),
                precision=HIGHEST, preferred_element_type=jnp.float32,
            )
            held_ref[stop:, stop:] -= lax.dot_general(
                panel, panel, (((1,), (1,)), ((), ())),
                precision=HIGHEST, preferred_element_type=jnp.float32,
            )
            if start:
                held_ref[stop:, :start] -= jnp.dot(
                    panel, before, precision=HIGHEST, preferred_element_type=jnp.float32
                )
            held_ref[stop:, start:stop] = -jnp.dot(
                panel, inverse, precision=HIGHEST, preferred_element_type=jnp.float32
            )
            held_ref[start:stop, stop:] = jnp.zeros((edge, size - stop), jnp.float32)
    first = pl.multiple_of(col_ref[0] * width, width)
    own = held_ref[pl.ds(first, width), :]
    high = own.astype(jnp.bfloat16)
    rest = own - high.astype(jnp.float32)
    middle = rest.astype(jnp.bfloat16)
    low = (rest - middle.astype(jnp.float32)).astype(jnp.bfloat16)
    total = jnp.zeros(out_ref.shape, jnp.float32)
    for piece in (low, middle, high):
        total += lax.dot_general(
            rows_ref[...], piece, (((1,), (1,)), ((), ())), preferred_element_type=jnp.float32
        )
    out_ref[...] = total


def from_partner(x, axis, apart):
    return lax.ppermute(x, axis, [(i, i ^ 1 << apart) for i in range(lax.axis_size(axis))])


def gram_of(row_block):
    return lax.dot_general(
        row_block, row_block, (((0,), (0,)), ((), ())), preferred_element_type=jnp.float32
    )


def local(tiles, tile_rows, tile_cols, tile_count, sketch, variant_scale):
    width = sketch.shape[1]
    edge = tiles.shape[1]
    owners = lax.axis_size("blk")
    own_blocks = sketch.shape[0] // edge
    own_rows = RB_DEV
    live_count = tile_count[0]
    every_slot = jnp.arange(tiles.shape[0], dtype=jnp.int32)
    owner_ids = jnp.arange(owners, dtype=jnp.int32)
    slot_owner = tile_cols // own_blocks
    slot_hits = (slot_owner[None, :] == owner_ids[:, None]) & (every_slot < live_count)[None, :]
    wanted = jnp.max(jnp.where(slot_hits, (tile_cols % own_blocks)[None, :], 0), axis=1)
    asked_blocks = lax.all_to_all(
        wanted.reshape(owners, 1), "blk", split_axis=0, concat_axis=0, tiled=True
    ).reshape(owners)

    own_scale = variant_scale.astype(jnp.float32)
    asked_scale = jnp.take(own_scale.reshape(own_blocks, edge), asked_blocks, axis=0)
    asked_sketch = jnp.take(sketch.reshape(own_blocks, edge, width), asked_blocks, axis=0)
    served = (asked_scale[:, :, None] * asked_sketch.astype(jnp.float32)).astype(jnp.bfloat16)
    fetched_sketch = lax.all_to_all(served, "blk", split_axis=0, concat_axis=0, tiled=True)

    panel = (owners, edge, width)
    group_terms = pl.pallas_call(
        range_kernel,
        out_shape=jax.ShapeDtypeStruct(panel, jnp.bfloat16),
        in_specs=[SMEM_SPEC] * 3 + [VMEM_SPEC] * 2,
        out_specs=VMEM_SPEC,
        scratch_shapes=[
            pltpu.VMEM((own_rows, edge, width), jnp.float32),
            pltpu.VMEM((own_rows, edge, width), jnp.bfloat16),
            pltpu.VMEM(panel, jnp.float32),
        ],
        compiler_params=PARAMS,
        name="range_terms",
    )(tile_rows, slot_owner, tile_count, tiles, fetched_sketch)
    arrived_terms = lax.all_to_all(group_terms, "blk", split_axis=0, concat_axis=0, tiled=True)
    squares = jnp.broadcast_to((asked_scale * asked_scale)[:, :, None], (owners, edge, edge))
    weighted = pl.pallas_call(
        weight_kernel,
        out_shape=jax.ShapeDtypeStruct(panel, jnp.bfloat16),
        in_specs=[SMEM_SPEC] + [VMEM_SPEC] * 2,
        out_specs=VMEM_SPEC,
        scratch_shapes=[pltpu.VMEM((own_blocks, edge, width), jnp.float32)],
        compiler_params=PARAMS,
        name="weighted_rows",
    )(asked_blocks, squares, arrived_terms)
    fetched_weighted = lax.all_to_all(weighted, "blk", split_axis=0, concat_axis=0, tiled=True)
    power_rows = pl.pallas_call(
        power_kernel,
        out_shape=jax.ShapeDtypeStruct((own_rows, edge, width), jnp.bfloat16),
        in_specs=[SMEM_SPEC] * 3 + [VMEM_SPEC] * 2,
        out_specs=VMEM_SPEC,
        scratch_shapes=[pltpu.VMEM((own_rows, edge, width), jnp.float32)],
        compiler_params=PARAMS,
        name="power_rows",
    )(tile_rows, slot_owner, tile_count, tiles, fetched_weighted)
    power_rows = power_rows.reshape(own_rows * edge, width)

    total_rows = own_rows * edge * owners
    partner_half = from_partner(power_rows, "col", 0)
    col_index = lax.axis_index("col")
    all_columns = jnp.where(
        col_index == 0,
        jnp.concatenate([power_rows, partner_half], axis=1),
        jnp.concatenate([partner_half, power_rows], axis=1),
    )
    gram_matrix = lax.psum(gram_of(all_columns), "blk") / total_rows
    size = gram_matrix.shape[0]
    return pl.pallas_call(
        basis_kernel,
        out_shape=jax.ShapeDtypeStruct((own_rows * edge, width), jnp.float32),
        in_specs=[SMEM_SPEC] + [VMEM_SPEC] * 2,
        out_specs=VMEM_SPEC,
        scratch_shapes=[pltpu.VMEM((size, size), jnp.float32)],
        compiler_params=PARAMS,
        name="basis_rows",
    )(col_index.reshape(1).astype(jnp.int32), gram_matrix, all_columns)


def solution(mesh):
    placed = (P("blk", None, None), P("blk"), P("blk"), P("blk"), P("blk", "col"), P("blk"))
    return jax.shard_map(
        local, mesh=mesh, in_specs=placed, out_specs=P("blk", "col"), check_vma=False
    )
```

time: 447 us -> 263 us (0.59); the launches traced: 441 us -> 262 us
  other arithmetic: 148 us -> 5.91 us
  blocking collectives: 0 us -> 90 us
  waiting for transfers between devices: 183 us -> 107 us
  starting transfers between devices: 47.4 us -> 8.93 us
  Pallas kernels: 0 us -> 31.5 us
  matrix products: 23.9 us -> 1.44 us
  local copies, waits for them, and re-layouts: 20 us -> 3.21 us
    another operation x17 -> x0, other arithmetic: 123 us -> none  [the longest x14 82.5 us: invert_factor(): lower_factor = jnp.linalg.cholesky(gram_matrix)]
    all_to_all x0 -> x3, blocking collectives: none -> 90 us  [the longest x1 32 us: local(): lax.all_to_all(group_terms, 'blk', split_axis=0, concat_axis=0, tiled=True)]
    all_to_all x3 -> x0, waiting for transfers between devices: 68.6 us -> none  [the longest x1 22.9 us: local(): lax.all_to_all(serve_blocks(weighted_own), 'blk', split_axis=0, concat_ax...]
    all_to_all x3 -> x0, starting transfers between devices: 38.4 us -> none  [the longest x1 27.9 us: local(): lax.all_to_all(group_terms, 'blk', split_axis=0, concat_axis=0, tiled=True)]
    pallas_call x0 -> x4, Pallas kernels: none -> 31.5 us  [the longest x1 22.3 us: local(): pl.pallas_call(basis_kernel, out_shape=jax.ShapeDtypeStruct((own_rows * e...]
    dot_general x11 -> x0, matrix products: 14.1 us -> none  [the longest x6 7.18 us: forward_step(): jnp.einsum('tij,tjk->tik', tile_group, selected, preferred_element_type=j...]
    psum x1, waiting for transfers between devices: 106 us -> 93.9 us  [local(): gram_matrix = lax.psum(gram_of(all_columns), 'blk') / total_rows]
    another operation x19 -> x0, local copies, waits for them, and re-layouts: 10.8 us -> none
  transfers between devices with their start and end apart: 6 -> 3, of which waited for: 6 -> 3; matrix products, arithmetic and copies ran while one was open for 1% -> 0% of each run, Pallas kernels for 0% -> 0%
where the time goes in v1:
time: 263 us; the launch traced here: 262 us
  waiting for transfers between devices  107 us (41%)
  blocking collectives  90 us (34%)
  Pallas kernels  31.5 us (12%)
  between operations  14.2 us (5%)
  starting transfers between devices  8.93 us (3%)
  other arithmetic  5.91 us (2%)
  local copies, waits for them, and re-layouts  3.21 us (1%)
    psum x1, waiting for transfers between devices, local(): gram_matrix = lax.psum(gram_of(all_columns), 'blk') / total_rows  93.9 us
    all_to_all x1, blocking collectives, local(): lax.all_to_all(group_terms, 'blk', split_axis=0, concat_axis=0, tiled=True)  32 us
    all_to_all x1, blocking collectives, local(): lax.all_to_all(weighted, 'blk', split_axis=0, concat_axis=0, tiled=True)  29.9 us
    all_to_all x1, blocking collectives, local(): lax.all_to_all(served, 'blk', split_axis=0, concat_axis=0, tiled=True)  28.1 us
    pallas_call x1, Pallas kernels, local(): pl.pallas_call(basis_kernel, out_shape=jax.ShapeDtypeStruct((own_rows * e...  22.3 us
    ppermute x1, waiting for transfers between devices, from_partner(): lax.ppermute(x, axis, [(i, i ^ 1 << apart) for i in range(lax.axis_size(a...  7.66 us
    all_to_all x1, starting transfers between devices, local(): lax.all_to_all(wanted.reshape(owners, 1), 'blk', split_axis=0, concat_axi...  7.36 us
    all_to_all x1, waiting for transfers between devices, local(): lax.all_to_all(wanted.reshape(owners, 1), 'blk', split_axis=0, concat_axi...  5.58 us
  transfers between devices with their start and end apart: 3, of which 3 were waited for; matrix products, arithmetic and copies ran while one was open for 0% of the time, Pallas kernels for 0%

profile of v1, /device:TPU:0, one launch (start us, length us, event | category | flops | bytes accessed | tf_op | source)
XLA Modules:
  0.0 262.2 jit_solution(3233762489538749545)
XLA Ops:
  6.5 0.0 copy-start
  6.5 0.8 and_select_fusion
  7.4 0.0 copy-start.2
  8.0 0.1 select_reduce_fusion
  8.1 0.7 copy.9
  8.8 7.4 %all-to-all-start = ((s32[16,1,1]{2,1,0:T(1,128)}), s32[16,1,1]{2,1,0:T(1,128)S(1)}, u32[]{:S(2)}, u32[]{:S(2)}) async-start(s32[16,1,1]{2,1,0:T(1,128)} %copy.9), calls=%async_computation | async-start | bytes 16384 | tf_op jit(solution)/shard_map/all_to_all | solution.py:204
  16.2 0.0 all-reduce.2.cloned.1.call-start
  16.2 0.7 bitcast_convert_fusion
  16.9 5.6 %all-to-all-done = s32[16,1,1]{2,1,0:T(1,128)S(1)} async-done(((s32[16,1,1]{2,1,0:T(1,128)}), s32[16,1,1]{2,1,0:T(1,128)S(1)}, u32[]{:S(2)}, u32[]{:S(2)}) %all-to-all-start) | async-done | bytes 96 | tf_op jit(solution)/shard_map/all_to_all | solution.py:204
  22.5 0.4 reduce.asked_ref
  22.9 0.0 copy-start.3
  22.9 0.6 gather_fusion
  23.5 0.0 copy-done
  23.5 0.6 gather_fusion.1
  24.1 0.1 fusion.2
  24.2 0.4 multiply_convert_fusion
  24.6 0.0 copy-done.2
  24.6 0.0 copy-done.3
  24.6 28.1 %all_to_all.27.fetched_ref = bf16[16,128,256]{2,1,0:T(8,128)(2,1)} all-to-all(bf16[16,128,256]{2,1,0:T(8,128)(2,1)S(1)} %multiply_convert_fusion), channel_id=1, replica_groups=mesh['blk'=16,'col'=2] {'blk'}, dimensions={0} | all-to-all | bytes 2097152 | tf_op jit(solution)/shard_map/all_to_all | solution.py:212
  52.7 3.2 %range_terms.1 = bf16[16,128,256]{2,1,0:T(8,128)(2,1)} custom-call(s32[24]{0:T(128)} %rows_ref.3, s32[24]{0:T(128)} %copy-done.2, s32[1]{0:T(128)} %copy.11.count_ref, bf16[24,128,128]{2,1,0:T(8,128)(2,1)} %tiles_ref.3, bf16[16,128,256]{2,1,0:T(8,128)(2,1)} %all_to_all.27.fetched_ref), custom_call_target="tpu_custom_call" | custom-call | tf_op jit(solution)/shard_map/range_terms/pallas_call | solution.py:215
  55.9 32.0 %all_to_all.28.terms_ref = bf16[16,128,256]{2,1,0:T(8,128)(2,1)} all-to-all(bf16[16,128,256]{2,1,0:T(8,128)(2,1)} %range_terms.1), channel_id=1, replica_groups=mesh['blk'=16,'col'=2] {'blk'}, dimensions={0} | all-to-all | bytes 2097152 | tf_op jit(solution)/shard_map/all_to_all | solution.py:228
  87.9 1.3 broadcast_in_dim.47.square_ref
  89.2 3.3 %weighted_rows.1 = bf16[16,128,256]{2,1,0:T(8,128)(2,1)} custom-call(s32[16]{0:T(128)} %copy-done.3, f32[16,128,128]{2,1,0:T(8,128)} %broadcast_in_dim.47.square_ref, bf16[16,128,256]{2,1,0:T(8,128)(2,1)} %all_to_all.28.terms_ref), custom_call_target="tpu_custom_call" | custom-call | tf_op jit(solution)/shard_map/weighted_rows/pallas_call | solution.py:230
  92.5 29.9 %all_to_all.29.fetched_ref = bf16[16,128,256]{2,1,0:T(8,128)(2,1)} all-to-all(bf16[16,128,256]{2,1,0:T(8,128)(2,1)} %weighted_rows.1), channel_id=1, replica_groups=mesh['blk'=16,'col'=2] {'blk'}, dimensions={0} | all-to-all | bytes 2097152 | tf_op jit(solution)/shard_map/all_to_all | solution.py:239
  122.5 2.6 %power_rows.1 = bf16[4,128,256]{2,1,0:T(8,128)(2,1)} custom-call(s32[24]{0:T(128)} %rows_ref.3, s32[24]{0:T(128)} %copy-done.2, s32[1]{0:T(128)} %copy.11.count_ref, bf16[24,128,128]{2,1,0:T(8,128)(2,1)} %tiles_ref.3, bf16[16,128,256]{2,1,0:T(8,128)(2,1)} %all_to_all.29.fetched_ref), custom_call_target="tpu_custom_call" | custom-call | tf_op jit(solution)/shard_map/power_rows/pallas_call | solution.py:240
  125.1 1.5 collective-permute-start
  126.6 7.7 %collective-permute-done = bf16[512,256]{1,0:T(8,128)(2,1)S(1)} collective-permute-done((bf16[512,256]{1,0:T(8,128)(2,1)}, bf16[512,256]{1,0:T(8,128)(2,1)S(1)}, u32[]{:S(2)}, u32[]{:S(2)}) %collective-permute-start) | collective-permute-done | bytes 262176 | tf_op jit(solution)/shard_map/ppermute | solution.py:183
  134.3 1.2 maximum_select_fusion.rows_ref
  135.4 0.0 copy-start.1
  135.5 1.4 fusion.3
  136.9 0.0 all-reduce.2.cloned.1.call-update
  136.9 93.9 %all-reduce.2.cloned.1.call-done = f32[512,512]{1,0:T(8,128)} async-done(((f32[512,512]{1,0:T(8,128)}), f32[512,512]{1,0:T(8,128)}) %all-reduce.2.cloned.1.call-update) | async-done | bytes 1048592 | tf_op jit(solution)/shard_map/psum | solution.py:259
  230.8 2.3 broadcast_multiply_fusion.gram_ref
  233.1 0.0 copy-done.1
  233.1 22.3 %basis_rows.1 = f32[512,256]{1,0:T(8,128)} custom-call(s32[1]{0:T(128)} %bitcast.col_ref, f32[512,512]{1,0:T(8,128)} %broadcast_multiply_fusion.gram_ref, bf16[512,512]{1,0:T(8,128)(2,1)} %copy-done.1), custom_call_target="tpu_custom_call" | custom-call | tf_op jit(solution)/shard_map/basis_rows/pallas_call | solution.py:261
  (4 shorter events, 0.0 us)
Async XLA Ops:
  6.5 17.0 %copy-start = (bf16[4096,256]{1,0:T(8,128)(2,1)S(1)}, bf16[4096,256]{1,0:T(8,128)(2,1)}, u32[]{:S(2)}) copy-start(bf16[4096,256]{1,0:T(8,128)(2,1)} %param.10) | copy-start | bytes 6291460
  7.4 17.2 %copy-start.2 = (s32[24]{0:T(128)}, s32[24]{0:T(128)S(1)}, u32[]{:S(2)}) copy-start(s32[24]{0:T(128)S(1)} %get-tuple-element.8.owner_ref) | copy-start | bytes 292
  8.8 13.7 %all-to-all-start = ((s32[16,1,1]{2,1,0:T(1,128)}), s32[16,1,1]{2,1,0:T(1,128)S(1)}, u32[]{:S(2)}, u32[]{:S(2)}) async-start(s32[16,1,1]{2,1,0:T(1,128)} %copy.9), calls=%async_computation | async-start | bytes 16384 | tf_op jit(solution)/shard_map/all_to_all | solution.py:204
  16.2 214.6 %all-reduce.2.cloned.1.call-start = ((), (), s32[]{:S(2)}) async-start(), calls=%async_computation.4 | async-start | bytes 2097152 | tf_op jit(solution)/shard_map/psum | solution.py:259
  22.9 1.7 copy-start.3
  125.1 9.2 %collective-permute-start = (bf16[512,256]{1,0:T(8,128)(2,1)}, bf16[512,256]{1,0:T(8,128)(2,1)S(1)}, u32[]{:S(2)}, u32[]{:S(2)}) collective-permute-start(bf16[512,256]{1,0:T(8,128)(2,1)} %bitcast.16), channel_id=1, source_target_pairs={{0,1},{1,0},{2,3},{3,2},{4,5},{5,4},{6,7},{7,6},{8,9},{9,8},{10,11... | collective-permute-start | bytes 786440 | tf_op jit(solution)/shard_map/ppermute | solution.py:183
  135.4 97.6 %copy-start.1 = (bf16[512,512]{1,0:T(8,128)(2,1)}, bf16[512,512]{1,0:T(8,128)(2,1)S(1)}, u32[]{:S(2)}) copy-start(bf16[512,512]{1,0:T(8,128)(2,1)S(1)} %maximum_select_fusion.rows_ref) | copy-start | bytes 1572868
Sparse Core Ops, SparseCore 0:
  137.0 93.6 all-reduce.1

commit v2 on v1

--- a/solution.py
+++ b/solution.py
@@ -133,11 +133,15 @@
     return jnp.concatenate(done, axis=0)
 
 
-def basis_kernel(col_ref, gram_ref, rows_ref, out_ref, held_ref):
-    size = gram_ref.shape[0]
+def basis_kernel(col_ref, blocks_ref, own_ref, other_ref, out_ref, held_ref):
     width = out_ref.shape[1]
-    edge = 128
-    held_ref[...] = gram_ref[...]
+    edge = blocks_ref.shape[2]
+    half = width // edge
+    size = 2 * width
+    for block_row, block_col, holder, index in block_places(half):
+        held_ref[
+            block_row * edge : (block_row + 1) * edge, block_col * edge : (block_col + 1) * edge
+        ] = blocks_ref[holder, index * edge : (index + 1) * edge, :]
     for start in range(0, size, edge):
         stop = start + edge
         inverse = invert_block(held_ref[start:stop, start:stop])
@@ -165,28 +169,185 @@
                 panel, inverse, precision=HIGHEST, preferred_element_type=jnp.float32
             )
             held_ref[start:stop, stop:] = jnp.zeros((edge, size - stop), jnp.float32)
-    first = pl.multiple_of(col_ref[0] * width, width)
-    own = held_ref[pl.ds(first, width), :]
-    high = own.astype(jnp.bfloat16)
-    rest = own - high.astype(jnp.float32)
-    middle = rest.astype(jnp.bfloat16)
-    low = (rest - middle.astype(jnp.float32)).astype(jnp.bfloat16)
-    total = jnp.zeros(out_ref.shape, jnp.float32)
-    for piece in (low, middle, high):
-        total += lax.dot_general(
-            rows_ref[...], piece, (((1,), (1,)), ((), ())), preferred_element_type=jnp.float32
+
+    def add_half(rows_ref, first):
+        own = held_ref[pl.ds(pl.multiple_of(col_ref[0] * width, width), width), first : first + width]
+        high = own.astype(jnp.bfloat16)
+        rest = own - high.astype(jnp.float32)
+        middle = rest.astype(jnp.bfloat16)
+        low = (rest - middle.astype(jnp.float32)).astype(jnp.bfloat16)
+        total = jnp.zeros(out_ref.shape, jnp.float32)
+        for piece in (low, middle, high):
+            total += lax.dot_general(
+                rows_ref[...], piece, (((1,), (1,)), ((), ())),
+                preferred_element_type=jnp.float32,
+            )
+        return total
+
+    @pl.when(col_ref[0] == 0)
+    def _():
+        out_ref[...] = add_half(own_ref, 0)
+
+    @pl.when(col_ref[0] != 0)
+    def _():
+        out_ref[...] = add_half(other_ref, 0) + add_half(own_ref, width)
+
+
+def block_places(half):
+    places = []
+    for holder in range(2):
+        index = 0
+        for block_col in range(half):
+            for block_row in range(block_col, half):
+                places.append((holder * half + block_row, holder * half + block_col, holder, index))
+                index += 1
+        for block_col in range(half // 2):
+            for block_row in range(half):
+                places.append(
+                    (half + block_row, holder * (half // 2) + block_col, holder, index)
+                )
+                index += 1
+    return places
+
+
+def gram_kernel(
+    owners, total_rows, chunk, own_ref, other_ref, blocks_ref,
+    part_ref, inbox_ref, pair_sems, part_send, part_recv, sum_send, sum_recv, pass_send, pass_recv,
+):
+    me = lax.axis_index("blk")
+    col = lax.axis_index("col")
+    partner = {"blk": me, "col": 1 - col}
+    width = own_ref.shape[1]
+    edge = blocks_ref.shape[2]
+    half = width // edge
+    own_depth = edge * half * (half + 1) // 2
+    depth = edge * (half * (half + 1) // 2 + half * half // 2)
+    reducers = (depth + chunk - 1) // chunk
+    early = own_depth // chunk
+
+    barrier = pltpu.get_barrier_semaphore()
+
+    def greet(d, carry):
+        pl.semaphore_signal(
+            barrier, inc=1, device_id={"blk": lax.rem(me + d, owners), "col": col},
+            device_id_type=pl.DeviceIdType.MESH,
         )
-    out_ref[...] = total
-
-
-def from_partner(x, axis, apart):
-    return lax.ppermute(x, axis, [(i, i ^ 1 << apart) for i in range(lax.axis_size(axis))])
-
-
-def gram_of(row_block):
-    return lax.dot_general(
-        row_block, row_block, (((0,), (0,)), ((), ())), preferred_element_type=jnp.float32
+        return carry
+
+    lax.fori_loop(1, owners, greet, 0)
+    pl.semaphore_signal(barrier, inc=1, device_id=partner, device_id_type=pl.DeviceIdType.MESH)
+    pl.semaphore_wait(barrier, owners)
+
+    def rows_of(q):
+        return pl.ds(pl.multiple_of(q * chunk, chunk), chunk)
+
+    def remote(src, dst, send_sem, recv_sem, device):
+        return pltpu.make_async_remote_copy(
+            src_ref=src, dst_ref=dst, send_sem=send_sem, recv_sem=recv_sem,
+            device_id=device, device_id_type=pl.DeviceIdType.MESH,
+        )
+
+    def peer(q):
+        return {"blk": q, "col": col}
+
+    def part_copy(src, q):
+        return remote(
+            part_ref.at[rows_of(q)], inbox_ref.at[src], part_send.at[q], part_recv.at[src], peer(q)
+        )
+
+    def sum_copy(src, q):
+        rows = blocks_ref.at[col, rows_of(src)]
+        return remote(rows, rows, sum_send.at[q], sum_recv.at[src], peer(q))
+
+    def pass_copy(holder, q):
+        rows = blocks_ref.at[holder, rows_of(q)]
+        return remote(rows, rows, pass_send.at[q], pass_recv.at[q], partner)
+
+    def each_peer(step, low, high):
+        def turn(d, carry):
+            q = lax.rem(me + d, owners)
+
+            @pl.when((q >= low) & (q < high))
+            def _():
+                step(q)
+
+            return carry
+
+        lax.fori_loop(1, owners, turn, 0)
+
+    pair = remote(own_ref, other_ref, pair_sems.at[0], pair_sems.at[1], partner)
+    pair.start()
+
+    own = own_ref[...]
+    own_gram = lax.dot_general(
+        own, own, (((0,), (0,)), ((), ())), preferred_element_type=jnp.float32
     )
+    index = 0
+    for block_col in range(half):
+        for block_row in range(block_col, half):
+            part_ref[index * edge : (index + 1) * edge, :] = own_gram[
+                block_row * edge : (block_row + 1) * edge, block_col * edge : (block_col + 1) * edge
+            ]
+            index += 1
+    each_peer(lambda q: part_copy(me, q).start(), 0, early)
+
+    pair.wait()
+    other = other_ref[...]
+    low_half = jnp.where(col == 0, own, other)
+    high_half = jnp.where(col == 0, other, own)
+    span = width // 2
+    low_part = jnp.where(col == 0, low_half[:, :span], low_half[:, span:])
+    cross = lax.dot_general(
+        high_half, low_part, (((0,), (0,)), ((), ())), preferred_element_type=jnp.float32
+    )
+    for block_col in range(half // 2):
+        for block_row in range(half):
+            part_ref[index * edge : (index + 1) * edge, :] = cross[
+                block_row * edge : (block_row + 1) * edge, block_col * edge : (block_col + 1) * edge
+            ]
+            index += 1
+    each_peer(lambda q: part_copy(me, q).start(), early, reducers)
+
+    @pl.when(me < reducers)
+    def _():
+        def add(d, total):
+            src = lax.rem(me + owners - d, owners)
+            part_copy(src, me).wait_recv()
+            return total + inbox_ref[src]
+
+        total = lax.fori_loop(1, owners, add, part_ref[rows_of(me)])
+        blocks_ref[col, rows_of(me)] = total / total_rows
+
+        def send(d, carry):
+            sum_copy(me, lax.rem(me + d, owners)).start()
+            return carry
+
+        lax.fori_loop(1, owners, send, 0)
+        pass_copy(col, me).start()
+
+    def hand_on(d, carry):
+        src = lax.rem(me + owners - d, owners)
+
+        @pl.when(src < reducers)
+        def _():
+            sum_copy(src, src).wait_recv()
+            pass_copy(col, src).start()
+
+        return carry
+
+    lax.fori_loop(1, owners, hand_on, 0)
+
+    def finish(q, carry):
+        pass_copy(1 - col, q).wait_recv()
+        pass_copy(col, q).wait_send()
+        return carry
+
+    lax.fori_loop(0, reducers, finish, 0)
+    each_peer(lambda q: part_copy(me, q).wait_send(), 0, reducers)
+
+    @pl.when(me < reducers)
+    def _():
+        each_peer(lambda q: sum_copy(me, q).wait_send(), 0, owners)
 
 
 def local(tiles, tile_rows, tile_cols, tile_count, sketch, variant_scale):
@@ -249,24 +410,38 @@
     power_rows = power_rows.reshape(own_rows * edge, width)
 
     total_rows = own_rows * edge * owners
-    partner_half = from_partner(power_rows, "col", 0)
-    col_index = lax.axis_index("col")
-    all_columns = jnp.where(
-        col_index == 0,
-        jnp.concatenate([power_rows, partner_half], axis=1),
-        jnp.concatenate([partner_half, power_rows], axis=1),
-    )
-    gram_matrix = lax.psum(gram_of(all_columns), "blk") / total_rows
-    size = gram_matrix.shape[0]
+    half = width // edge
+    depth = edge * (half * (half + 1) // 2 + half * half // 2)
+    chunk = -(-depth // (8 * owners)) * 8
+    reducers = -(-depth // chunk)
+    other_rows, blocks = pl.pallas_call(
+        functools.partial(gram_kernel, owners, total_rows, chunk),
+        out_shape=(
+            jax.ShapeDtypeStruct(power_rows.shape, jnp.bfloat16),
+            jax.ShapeDtypeStruct((2, reducers * chunk, edge), jnp.float32),
+        ),
+        in_specs=[VMEM_SPEC],
+        out_specs=(VMEM_SPEC, VMEM_SPEC),
+        scratch_shapes=[
+            pltpu.VMEM((reducers * chunk, edge), jnp.float32),
+            pltpu.VMEM((owners, chunk, edge), jnp.float32),
+            pltpu.SemaphoreType.DMA((2,)),
+        ]
+        + [pltpu.SemaphoreType.DMA((owners,))] * 6,
+        compiler_params=pltpu.CompilerParams(
+            vmem_limit_bytes=VMEM_BYTES, collective_id=0, has_side_effects=True
+        ),
+        name="gram_blocks",
+    )(power_rows)
     return pl.pallas_call(
         basis_kernel,
         out_shape=jax.ShapeDtypeStruct((own_rows * edge, width), jnp.float32),
-        in_specs=[SMEM_SPEC] + [VMEM_SPEC] * 2,
+        in_specs=[SMEM_SPEC] + [VMEM_SPEC] * 3,
         out_specs=VMEM_SPEC,
-        scratch_shapes=[pltpu.VMEM((size, size), jnp.float32)],
+        scratch_shapes=[pltpu.VMEM((2 * width, 2 * width), jnp.float32)],
         compiler_params=PARAMS,
         name="basis_rows",
-    )(col_index.reshape(1).astype(jnp.int32), gram_matrix, all_columns)
+    )(lax.axis_index("col").reshape(1).astype(jnp.int32), blocks, power_rows, other_rows)
 
 
 def solution(mesh):

time: 263 us -> 183 us (0.70)
  waiting for transfers between devices: 107 us -> 28.6 us
  Pallas kernels: 31.5 us -> 72.8 us
  blocking collectives: 90 us -> 60.1 us
  between operations: 14.2 us -> 0.77 us
  other arithmetic: 5.91 us -> 2.47 us
  starting transfers between devices: 8.93 us -> 12.3 us
    psum x1 -> x0, waiting for transfers between devices: 93.9 us -> none  [local(): gram_matrix = lax.psum(gram_of(all_columns), 'blk') / total_rows]
    pallas_call x0 -> x1, Pallas kernels: none -> 41.9 us  [local(): pl.pallas_call(functools.partial(gram_kernel, owners, total_rows, chunk),...]
    all_to_all x1 -> x0, blocking collectives: 29.9 us -> none  [local(): lax.all_to_all(weighted, 'blk', split_axis=0, concat_axis=0, tiled=True)]
    all_to_all x0 -> x1, waiting for transfers between devices: none -> 22.9 us  [local(): lax.all_to_all(weighted, 'blk', split_axis=0, concat_axis=0, tiled=True)]
    ppermute x1 -> x0, waiting for transfers between devices: 7.66 us -> none  [from_partner(): lax.ppermute(x, axis, [(i, i ^ 1 << apart) for i in range(lax.axis_size(a...]
    all_to_all x0 -> x1, starting transfers between devices: none -> 4.9 us  [local(): lax.all_to_all(weighted, 'blk', split_axis=0, concat_axis=0, tiled=True)]
  transfers between devices with their start and end apart: 3 -> 2, of which waited for: 3 -> 2; matrix products, arithmetic and copies ran while one was open for 0% -> 0% of each run, Pallas kernels for 0% -> 0%
where the time goes in v2:
time: 183 us; the launch traced here: 181 us
  Pallas kernels  72.8 us (40%)
  blocking collectives  60.1 us (33%)
  waiting for transfers between devices  28.6 us (16%)
  starting transfers between devices  12.3 us (7%)
  local copies, waits for them, and re-layouts  4.17 us (2%)
  other arithmetic  2.47 us (1%)
    pallas_call x1, Pallas kernels, local(): pl.pallas_call(functools.partial(gram_kernel, owners, total_rows, chunk),...  41.9 us
    all_to_all x1, blocking collectives, local(): lax.all_to_all(group_terms, 'blk', split_axis=0, concat_axis=0, tiled=True)  32 us
    all_to_all x1, blocking collectives, local(): lax.all_to_all(served, 'blk', split_axis=0, concat_axis=0, tiled=True)  28.1 us
    all_to_all x1, waiting for transfers between devices, local(): lax.all_to_all(weighted, 'blk', split_axis=0, concat_axis=0, tiled=True)  22.9 us
    pallas_call x1, Pallas kernels, local(): pl.pallas_call(basis_kernel, out_shape=jax.ShapeDtypeStruct((own_rows * e...  21.9 us
    all_to_all x1, starting transfers between devices, local(): lax.all_to_all(wanted.reshape(owners, 1), 'blk', split_axis=0, concat_axi...  7.36 us
    all_to_all x1, waiting for transfers between devices, local(): lax.all_to_all(wanted.reshape(owners, 1), 'blk', split_axis=0, concat_axi...  5.63 us
    all_to_all x1, starting transfers between devices, local(): lax.all_to_all(weighted, 'blk', split_axis=0, concat_axis=0, tiled=True)  4.9 us
  transfers between devices with their start and end apart: 2, of which 2 were waited for; matrix products, arithmetic and copies ran while one was open for 0% of the time, Pallas kernels for 0%

profile of v2, /device:TPU:0, one launch (start us, length us, event | category | flops | bytes accessed | tf_op | source)
XLA Modules:
  0.0 181.1 jit_solution(13981981036274295782)
XLA Ops:
  0.0 0.0 copy-start
  0.0 0.8 and_select_fusion
  0.8 0.0 copy-start.2
  1.5 0.1 select_reduce_fusion
  1.6 0.7 copy.9
  2.3 7.4 %all-to-all-start = ((s32[16,1,1]{2,1,0:T(1,128)}), s32[16,1,1]{2,1,0:T(1,128)S(1)}, u32[]{:S(2)}, u32[]{:S(2)}) async-start(s32[16,1,1]{2,1,0:T(1,128)} %copy.9), calls=%async_computation | async-start | bytes 16384 | tf_op jit(solution)/shard_map/all_to_all | solution.py:365
  9.7 0.7 bitcast_convert_fusion
  10.4 5.6 %all-to-all-done = s32[16,1,1]{2,1,0:T(1,128)S(1)} async-done(((s32[16,1,1]{2,1,0:T(1,128)}), s32[16,1,1]{2,1,0:T(1,128)S(1)}, u32[]{:S(2)}, u32[]{:S(2)}) %all-to-all-start) | async-done | bytes 96 | tf_op jit(solution)/shard_map/all_to_all | solution.py:365
  16.0 0.4 reduce.asked_ref
  16.4 0.0 copy-start.3
  16.4 0.6 gather_fusion
  17.0 0.0 copy-done
  17.0 0.6 gather_fusion.1
  17.6 0.1 fusion.2
  17.7 0.4 multiply_convert_fusion
  18.0 0.0 copy-done.2
  18.1 0.0 copy-done.3
  18.1 28.1 %all_to_all.27.fetched_ref = bf16[16,128,256]{2,1,0:T(8,128)(2,1)} all-to-all(bf16[16,128,256]{2,1,0:T(8,128)(2,1)S(1)} %multiply_convert_fusion), channel_id=1, replica_groups=mesh['blk'=16,'col'=2] {'blk'}, dimensions={0} | all-to-all | bytes 2097152 | tf_op jit(solution)/shard_map/all_to_all | solution.py:373
  46.2 3.3 %range_terms.1 = bf16[16,128,256]{2,1,0:T(8,128)(2,1)} custom-call(s32[24]{0:T(128)} %rows_ref.3, s32[24]{0:T(128)} %copy-done.2, s32[1]{0:T(128)} %copy.10.count_ref, bf16[24,128,128]{2,1,0:T(8,128)(2,1)} %tiles_ref.3, bf16[16,128,256]{2,1,0:T(8,128)(2,1)} %all_to_all.27.fetched_ref), custom_call_target="tpu_custom_call" | custom-call | tf_op jit(solution)/shard_map/range_terms/pallas_call | solution.py:376
  49.4 32.0 %all_to_all.28.terms_ref = bf16[16,128,256]{2,1,0:T(8,128)(2,1)} all-to-all(bf16[16,128,256]{2,1,0:T(8,128)(2,1)} %range_terms.1), channel_id=1, replica_groups=mesh['blk'=16,'col'=2] {'blk'}, dimensions={0} | all-to-all | bytes 2097152 | tf_op jit(solution)/shard_map/all_to_all | solution.py:389
  81.4 1.3 broadcast_in_dim.47.square_ref
  82.7 3.3 %weighted_rows.1 = bf16[16,128,256]{2,1,0:T(8,128)(2,1)} custom-call(s32[16]{0:T(128)} %copy-done.3, f32[16,128,128]{2,1,0:T(8,128)} %broadcast_in_dim.47.square_ref, bf16[16,128,256]{2,1,0:T(8,128)(2,1)} %all_to_all.28.terms_ref), custom_call_target="tpu_custom_call" | custom-call | tf_op jit(solution)/shard_map/weighted_rows/pallas_call | solution.py:391
  86.0 4.9 %all-to-all-start.3 = ((bf16[16,128,256]{2,1,0:T(8,128)(2,1)}), bf16[16,128,256]{2,1,0:T(8,128)(2,1)S(1)}, u32[]{:S(2)}, u32[]{:S(2)}) async-start(bf16[16,128,256]{2,1,0:T(8,128)(2,1)} %weighted_rows.1), calls=%async_computation.3 | async-start | bytes 2097152 | tf_op jit(solution)/shard_map/all_to_all | solution.py:400
  90.9 22.9 %all-to-all-done.3.fetched_ref = bf16[16,128,256]{2,1,0:T(8,128)(2,1)S(1)} async-done(((bf16[16,128,256]{2,1,0:T(8,128)(2,1)}), bf16[16,128,256]{2,1,0:T(8,128)(2,1)S(1)}, u32[]{:S(2)}, u32[]{:S(2)}) %all-to-all-start.3) | async-done | bytes 1048608 | tf_op jit(solution)/shard_map/all_to_all | solution.py:400
  113.9 0.0 copy-start.1
  113.9 1.0 copy-done.1
  114.8 2.4 %power_rows.1 = bf16[4,128,256]{2,1,0:T(8,128)(2,1)} custom-call(s32[24]{0:T(128)} %rows_ref.3, s32[24]{0:T(128)} %copy-done.2, s32[1]{0:T(128)} %copy.10.count_ref, bf16[24,128,128]{2,1,0:T(8,128)(2,1)} %tiles_ref.3, bf16[16,128,256]{2,1,0:T(8,128)(2,1)} %copy-done.1), custom_call_target="tpu_custom_call" | custom-call | tf_op jit(solution)/shard_map/power_rows/pallas_call | solution.py:401
  117.3 41.9 %gram_blocks.1 = (bf16[512,256]{1,0:T(8,128)(2,1)}, f32[2,640,128]{2,1,0:T(8,128)}) custom-call(bf16[512,256]{1,0:T(8,128)(2,1)} %bitcast.14), custom_call_target="tpu_custom_call" | custom-call | tf_op jit(solution)/shard_map/gram_blocks/pallas_call | solution.py:417
  159.2 21.9 %basis_rows.1 = f32[512,256]{1,0:T(8,128)} custom-call(s32[1]{0:T(128)} %bitcast.col_ref, f32[2,640,128]{2,1,0:T(8,128)} %get-tuple-element.7.blocks_ref, bf16[512,256]{1,0:T(8,128)(2,1)} %bitcast.15, bf16[512,256]{1,0:T(8,128)(2,1)} %get-tuple-element.8.other_ref), custom_call_target="tpu_custom_call" | custom-call | tf_op jit(solution)/shard_map/basis_rows/pallas_call | solution.py:436
  (4 shorter events, 0.0 us)
Async XLA Ops:
  0.0 17.0 %copy-start = (bf16[4096,256]{1,0:T(8,128)(2,1)S(1)}, bf16[4096,256]{1,0:T(8,128)(2,1)}, u32[]{:S(2)}) copy-start(bf16[4096,256]{1,0:T(8,128)(2,1)} %param.10) | copy-start | bytes 6291460
  0.8 17.2 %copy-start.2 = (s32[24]{0:T(128)}, s32[24]{0:T(128)S(1)}, u32[]{:S(2)}) copy-start(s32[24]{0:T(128)S(1)} %get-tuple-element.12.owner_ref) | copy-start | bytes 292
  2.3 13.7 %all-to-all-start = ((s32[16,1,1]{2,1,0:T(1,128)}), s32[16,1,1]{2,1,0:T(1,128)S(1)}, u32[]{:S(2)}, u32[]{:S(2)}) async-start(s32[16,1,1]{2,1,0:T(1,128)} %copy.9), calls=%async_computation | async-start | bytes 16384 | tf_op jit(solution)/shard_map/all_to_all | solution.py:365
  16.4 1.7 copy-start.3
  86.0 27.9 %all-to-all-start.3 = ((bf16[16,128,256]{2,1,0:T(8,128)(2,1)}), bf16[16,128,256]{2,1,0:T(8,128)(2,1)S(1)}, u32[]{:S(2)}, u32[]{:S(2)}) async-start(bf16[16,128,256]{2,1,0:T(8,128)(2,1)} %weighted_rows.1), calls=%async_computation.3 | async-start | bytes 2097152 | tf_op jit(solution)/shard_map/all_to_all | solution.py:400
  113.9 1.0 copy-start.1

commit v3 on v2

--- a/solution.py
+++ b/solution.py
@@ -8,7 +8,6 @@
 
 TPR = 6
 RB_DEV = 4
-STEP = 3
 PANEL = 8
 VMEM_BYTES = 60 * 2**20
 HIGHEST = lax.Precision.HIGHEST
@@ -18,76 +17,159 @@
 PARAMS = pltpu.CompilerParams(vmem_limit_bytes=VMEM_BYTES)
 
 
-def forward_rows(rows_ref, owner_ref, count, tiles_ref, fetched_ref, acc_ref):
-    acc_ref[...] = jnp.zeros_like(acc_ref)
-
-    def turn(index, carry):
-        slots = [index * STEP + step for step in range(STEP)]
-        products = [
-            jnp.dot(
-                tiles_ref[slot], fetched_ref[owner_ref[slot]], preferred_element_type=jnp.float32
-            )
-            for slot in slots
-        ]
-        for slot, product in zip(slots, products):
-            acc_ref[rows_ref[slot]] += product
+def exchange_kernel(
+    owners, slot_ref, wanted_ref, scale_ref, tiles_ref, sketch_ref, rows_ref,
+    asked_in, asked, tile_set, send, fetched, arrived, sums, squares, acc, held,
+    ask_sems, sketch_sems, term_sems, weight_sems, local_sem,
+):
+    me = lax.axis_index("blk")
+    col = lax.axis_index("col")
+    slots, edge, _ = tiles_ref.shape
+    width = sketch_ref.shape[2]
+    own_rows = acc.shape[0] // edge
+
+    barrier = pltpu.get_barrier_semaphore()
+
+    def each(step, first=1):
+        def turn(d, carry):
+            step(d)
+            return carry
+
+        lax.fori_loop(first, owners, turn, 0)
+
+    def ahead(d):
+        return lax.rem(me + d, owners)
+
+    def behind(d):
+        return lax.rem(me + owners - d, owners)
+
+    def greet(d):
+        pl.semaphore_signal(
+            barrier, inc=1, device_id={"blk": ahead(d), "col": col},
+            device_id_type=pl.DeviceIdType.MESH,
+        )
+
+    each(greet)
+
+    def copy_of(source, target, sems):
+        def make(src, q):
+            return pltpu.make_async_remote_copy(
+                src_ref=source.at[q], dst_ref=target.at[src],
+                send_sem=sems.at[0, q], recv_sem=sems.at[1, src],
+                device_id={"blk": q, "col": col}, device_id_type=pl.DeviceIdType.MESH,
+            )
+
+        return make
+
+    ask_copy = copy_of(wanted_ref, asked_in, ask_sems)
+    sketch_copy = copy_of(send, fetched, sketch_sems)
+    term_copy = copy_of(send, arrived, term_sems)
+    weight_copy = copy_of(send, fetched, weight_sems)
+
+    tile_set[:slots] = tiles_ref[...]
+    tile_set[slots] = jnp.zeros((edge, edge), jnp.bfloat16)
+    asked_in[me] = wanted_ref[me]
+    pl.semaphore_wait(barrier, owners - 1)
+    each(lambda d: ask_copy(me, ahead(d)).start())
+    each(lambda d: ask_copy(behind(d), me).wait_recv())
+    into_scalars = pltpu.make_async_copy(asked_in, asked, local_sem)
+    into_scalars.start()
+    into_scalars.wait()
+
+    lanes = lax.broadcasted_iota(jnp.int32, (edge, edge), 1)
+    sublanes = lax.broadcasted_iota(jnp.int32, (edge, edge), 0)
+    ones = jnp.ones((edge, edge), jnp.bfloat16)
+
+    def served(q):
+        block = asked[q, 0, 0]
+        spread = jnp.broadcast_to(scale_ref[block], (edge, edge))
+        diagonal = jnp.where(lanes == sublanes, spread, 0.0).astype(jnp.bfloat16)
+        column = jnp.dot(diagonal, ones, preferred_element_type=jnp.float32)
+        squares[q] = column * column
+        rows = sketch_ref[block].astype(jnp.float32)
+        return (rows * jnp.concatenate([column] * (width // edge), axis=1)).astype(jnp.bfloat16)
+
+    def serve(d):
+        q = ahead(d)
+        send[q] = served(q)
+        sketch_copy(me, q).start()
+
+    each(serve)
+    fetched[me] = served(me)
+
+    def stack_of(owner):
+        return jnp.concatenate(
+            [tile_set[slot_ref[owner * own_rows + row]] for row in range(own_rows)], axis=0
+        )
+
+    def forward(copies):
+        acc[...] = jnp.dot(stack_of(me), fetched[me], preferred_element_type=jnp.float32)
+
+        def take(d):
+            owner = behind(d)
+            copies(owner, me).wait_recv()
+            acc[...] += jnp.dot(
+                stack_of(owner), fetched[owner], preferred_element_type=jnp.float32
+            )
+
+        each(take)
+
+    forward(sketch_copy)
+    held[...] = acc[...].astype(jnp.bfloat16)
+    each(lambda d: sketch_copy(me, ahead(d)).wait_send())
+
+    def term_of(owner):
+        return lax.dot_general(
+            stack_of(owner), held[...], (((0,), (0,)), ((), ())),
+            preferred_element_type=jnp.float32,
+        ).astype(jnp.bfloat16)
+
+    def give(d):
+        q = ahead(d)
+        send[q] = term_of(q)
+        term_copy(me, q).start()
+
+    each(give)
+    arrived[me] = term_of(me)
+
+    def share(src, q):
+        same = (asked[src, 0, 0] == asked[q, 0, 0]).astype(jnp.float32)
+        return same * arrived[src].astype(jnp.float32)
+
+    def begin(q, carry):
+        sums[q] = share(me, q)
         return carry
 
-    lax.fori_loop(0, count // STEP, turn, 0)
-
-
-def range_kernel(rows_ref, owner_ref, count_ref, tiles_ref, fetched_ref, terms_ref, acc_ref, held_ref, sum_ref):
-    count = count_ref[0]
-    forward_rows(rows_ref, owner_ref, count, tiles_ref, fetched_ref, acc_ref)
-    held_ref[...] = acc_ref[...].astype(jnp.bfloat16)
-    sum_ref[...] = jnp.zeros_like(sum_ref)
-
-    def turn(index, carry):
-        slots = [index * STEP + step for step in range(STEP)]
-        products = [
-            lax.dot_general(
-                tiles_ref[slot],
-                held_ref[rows_ref[slot]],
-                (((0,), (0,)), ((), ())),
-                preferred_element_type=jnp.float32,
-            )
-            for slot in slots
-        ]
-        for slot, product in zip(slots, products):
-            sum_ref[owner_ref[slot]] += product
-        return carry
-
-    lax.fori_loop(0, count // STEP, turn, 0)
-    terms_ref[...] = sum_ref[...].astype(jnp.bfloat16)
-
-
-def power_kernel(rows_ref, owner_ref, count_ref, tiles_ref, fetched_ref, out_ref, acc_ref):
-    forward_rows(rows_ref, owner_ref, count_ref[0], tiles_ref, fetched_ref, acc_ref)
-    out_ref[...] = acc_ref[...].astype(jnp.bfloat16)
-
-
-def weight_kernel(asked_ref, square_ref, terms_ref, out_ref, sum_ref):
-    owners, edge, width = terms_ref.shape
-
-    def clear(q, carry):
-        sum_ref[asked_ref[q]] = jnp.zeros((edge, width), jnp.float32)
-        return carry
-
-    def gather(q, carry):
-        sum_ref[asked_ref[q]] += terms_ref[q].astype(jnp.float32)
-        return carry
-
-    def scale(q, carry):
-        total = sum_ref[asked_ref[q]]
-        for part in range(0, width, edge):
-            out_ref[q, :, part : part + edge] = (
-                square_ref[q] * total[:, part : part + edge]
-            ).astype(jnp.bfloat16)
-        return carry
-
-    lax.fori_loop(0, owners, clear, 0)
-    lax.fori_loop(0, owners, gather, 0)
-    lax.fori_loop(0, owners, scale, 0)
+    lax.fori_loop(0, owners, begin, 0)
+
+    def gather(d):
+        src = behind(d)
+        term_copy(src, me).wait_recv()
+
+        def add(q, carry):
+            sums[q] += share(src, q)
+            return carry
+
+        lax.fori_loop(0, owners, add, 0)
+
+    each(gather)
+    each(lambda d: term_copy(me, ahead(d)).wait_send())
+
+    def weighted(q):
+        square = jnp.concatenate([squares[q]] * (width // edge), axis=1)
+        return (square * sums[q]).astype(jnp.bfloat16)
+
+    def give_weighted(d):
+        q = ahead(d)
+        send[q] = weighted(q)
+        weight_copy(me, q).start()
+
+    each(give_weighted)
+    fetched[me] = weighted(me)
+    forward(weight_copy)
+    rows_ref[...] = acc[...].astype(jnp.bfloat16)
+    each(lambda d: ask_copy(me, ahead(d)).wait_send())
+    each(lambda d: weight_copy(me, ahead(d)).wait_send())
 
 
 def invert_block(block):
@@ -356,58 +438,47 @@
     owners = lax.axis_size("blk")
     own_blocks = sketch.shape[0] // edge
     own_rows = RB_DEV
-    live_count = tile_count[0]
-    every_slot = jnp.arange(tiles.shape[0], dtype=jnp.int32)
+    slots = tiles.shape[0]
+    every_slot = jnp.arange(slots, dtype=jnp.int32)
     owner_ids = jnp.arange(owners, dtype=jnp.int32)
+    live = every_slot < tile_count[0]
     slot_owner = tile_cols // own_blocks
-    slot_hits = (slot_owner[None, :] == owner_ids[:, None]) & (every_slot < live_count)[None, :]
+    slot_hits = (slot_owner[None, :] == owner_ids[:, None]) & live[None, :]
     wanted = jnp.max(jnp.where(slot_hits, (tile_cols % own_blocks)[None, :], 0), axis=1)
-    asked_blocks = lax.all_to_all(
-        wanted.reshape(owners, 1), "blk", split_axis=0, concat_axis=0, tiled=True
-    ).reshape(owners)
-
-    own_scale = variant_scale.astype(jnp.float32)
-    asked_scale = jnp.take(own_scale.reshape(own_blocks, edge), asked_blocks, axis=0)
-    asked_sketch = jnp.take(sketch.reshape(own_blocks, edge, width), asked_blocks, axis=0)
-    served = (asked_scale[:, :, None] * asked_sketch.astype(jnp.float32)).astype(jnp.bfloat16)
-    fetched_sketch = lax.all_to_all(served, "blk", split_axis=0, concat_axis=0, tiled=True)
-
+    places = jnp.arange(owners * own_rows, dtype=jnp.int32)
+    place_hits = ((slot_owner * own_rows + tile_rows)[None, :] == places[:, None]) & live[None, :]
+    slot_of = jnp.min(jnp.where(place_hits, every_slot[None, :], slots), axis=1)
     panel = (owners, edge, width)
-    group_terms = pl.pallas_call(
-        range_kernel,
-        out_shape=jax.ShapeDtypeStruct(panel, jnp.bfloat16),
-        in_specs=[SMEM_SPEC] * 3 + [VMEM_SPEC] * 2,
+    power_rows = pl.pallas_call(
+        functools.partial(exchange_kernel, owners),
+        out_shape=jax.ShapeDtypeStruct((own_rows * edge, width), jnp.bfloat16),
+        in_specs=[SMEM_SPEC] + [VMEM_SPEC] * 4,
         out_specs=VMEM_SPEC,
         scratch_shapes=[
-            pltpu.VMEM((own_rows, edge, width), jnp.float32),
-            pltpu.VMEM((own_rows, edge, width), jnp.bfloat16),
+            pltpu.VMEM((owners, 1, edge), jnp.int32),
+            pltpu.SMEM((owners, 1, edge), jnp.int32),
+            pltpu.VMEM((slots + 1, edge, edge), jnp.bfloat16),
+            pltpu.VMEM(panel, jnp.bfloat16),
+            pltpu.VMEM(panel, jnp.bfloat16),
+            pltpu.VMEM(panel, jnp.bfloat16),
             pltpu.VMEM(panel, jnp.float32),
-        ],
-        compiler_params=PARAMS,
-        name="range_terms",
-    )(tile_rows, slot_owner, tile_count, tiles, fetched_sketch)
-    arrived_terms = lax.all_to_all(group_terms, "blk", split_axis=0, concat_axis=0, tiled=True)
-    squares = jnp.broadcast_to((asked_scale * asked_scale)[:, :, None], (owners, edge, edge))
-    weighted = pl.pallas_call(
-        weight_kernel,
-        out_shape=jax.ShapeDtypeStruct(panel, jnp.bfloat16),
-        in_specs=[SMEM_SPEC] + [VMEM_SPEC] * 2,
-        out_specs=VMEM_SPEC,
-        scratch_shapes=[pltpu.VMEM((own_blocks, edge, width), jnp.float32)],
-        compiler_params=PARAMS,
-        name="weighted_rows",
-    )(asked_blocks, squares, arrived_terms)
-    fetched_weighted = lax.all_to_all(weighted, "blk", split_axis=0, concat_axis=0, tiled=True)
-    power_rows = pl.pallas_call(
-        power_kernel,
-        out_shape=jax.ShapeDtypeStruct((own_rows, edge, width), jnp.bfloat16),
-        in_specs=[SMEM_SPEC] * 3 + [VMEM_SPEC] * 2,
-        out_specs=VMEM_SPEC,
-        scratch_shapes=[pltpu.VMEM((own_rows, edge, width), jnp.float32)],
-        compiler_params=PARAMS,
-        name="power_rows",
-    )(tile_rows, slot_owner, tile_count, tiles, fetched_weighted)
-    power_rows = power_rows.reshape(own_rows * edge, width)
+            pltpu.VMEM((owners, edge, edge), jnp.float32),
+            pltpu.VMEM((own_rows * edge, width), jnp.float32),
+            pltpu.VMEM((own_rows * edge, width), jnp.bfloat16),
+        ]
+        + [pltpu.SemaphoreType.DMA((2, owners))] * 4
+        + [pltpu.SemaphoreType.DMA],
+        compiler_params=pltpu.CompilerParams(
+            vmem_limit_bytes=VMEM_BYTES, collective_id=1, has_side_effects=True
+        ),
+        name="exchange_rows",
+    )(
+        slot_of,
+        jnp.broadcast_to(wanted[:, None, None], (owners, 1, edge)),
+        variant_scale.astype(jnp.float32).reshape(own_blocks, 1, edge),
+        tiles,
+        sketch.reshape(own_blocks, edge, width),
+    )
 
     total_rows = own_rows * edge * owners
     half = width // edge

time: 183 us -> 154 us (0.84); the launches traced: 181 us -> 154 us
  Pallas kernels: 72.8 us -> 150 us
  blocking collectives: 60.1 us -> 0 us
  waiting for transfers between devices: 28.6 us -> 0 us
  starting transfers between devices: 12.3 us -> 0 us
  local copies, waits for them, and re-layouts: 4.17 us -> 0.68 us
    pallas_call x3 -> x1, Pallas kernels: 8.98 us -> 78.6 us  [local(): pl.pallas_call(functools.partial(exchange_kernel, owners), out_shape=jax....]
    all_to_all x2 -> x0, blocking collectives: 60.1 us -> none  [the longest x1 32 us: local(): lax.all_to_all(group_terms, 'blk', split_axis=0, concat_axis=0, tiled=True)]
    all_to_all x2 -> x0, waiting for transfers between devices: 28.6 us -> none  [the longest x1 22.9 us: local(): lax.all_to_all(weighted, 'blk', split_axis=0, concat_axis=0, tiled=True)]
    all_to_all x2 -> x0, starting transfers between devices: 12.3 us -> none  [the longest x1 7.36 us: local(): lax.all_to_all(wanted.reshape(owners, 1), 'blk', split_axis=0, concat_axi...]
    pallas_call x1, Pallas kernels: 41.9 us -> 49.4 us  [local(): pl.pallas_call(functools.partial(gram_kernel, owners, total_rows, chunk),...]
  transfers between devices with their start and end apart: 2 -> 0, of which waited for: 2 -> 0; matrix products, arithmetic and copies ran while one was open for 0% -> 0% of each run, Pallas kernels for 0% -> 0%
where the time goes in v3:
time: 154 us
  Pallas kernels  150 us (97%)
  other arithmetic  2.75 us (2%)
    pallas_call x1, Pallas kernels, local(): pl.pallas_call(functools.partial(exchange_kernel, owners), out_shape=jax....  78.6 us
    pallas_call x1, Pallas kernels, local(): pl.pallas_call(functools.partial(gram_kernel, owners, total_rows, chunk),...  49.4 us
    pallas_call x1, Pallas kernels, local(): pl.pallas_call(basis_kernel, out_shape=jax.ShapeDtypeStruct((own_rows * e...  21.9 us

profile of v3, /device:TPU:0, one launch (start us, length us, event | category | flops | bytes accessed | tf_op | source)
XLA Modules:
  0.0 154.0 jit_solution(8285493346863860343)
XLA Ops:
  0.7 0.7 multiply_add_fusion
  1.4 0.6 select_reduce_fusion.slot_ref
  2.0 0.1 select_reduce_fusion.1
  2.1 0.7 broadcast_in_dim.42.wanted_ref
  2.8 1.3 reshape.25
  4.1 78.6 %exchange_rows.1.own_ref = bf16[512,256]{1,0:T(8,128)(2,1)} custom-call(s32[64]{0:T(128)} %select_reduce_fusion.slot_ref, s32[16,1,128]{2,1,0:T(1,128)} %broadcast_in_dim.42.wanted_ref, f32[32,1,128]{2,1,0:T(1,128)} %bitcast.6, bf16[24,128,128]{2,1,0:T(8,128)(2,1)} %tiles_ref.1, bf16[32,128,256]{2,1,0:T(8,128)(2,1)} %bitcast.5), custom_call_target="tpu_custom_call" | custom-call | tf_op jit(solution)/shard_map/exchange_rows/pallas_call | solution.py:452
  82.7 49.4 %gram_blocks.1 = (bf16[512,256]{1,0:T(8,128)(2,1)}, f32[2,640,128]{2,1,0:T(8,128)}) custom-call(bf16[512,256]{1,0:T(8,128)(2,1)} %exchange_rows.1.own_ref), custom_call_target="tpu_custom_call" | custom-call | tf_op jit(solution)/shard_map/gram_blocks/pallas_call | solution.py:488
  132.1 21.9 %basis_rows.1 = f32[512,256]{1,0:T(8,128)} custom-call(s32[1]{0:T(128)} %bitcast.col_ref, f32[2,640,128]{2,1,0:T(8,128)} %get-tuple-element.7.blocks_ref, bf16[512,256]{1,0:T(8,128)(2,1)} %exchange_rows.1.own_ref, bf16[512,256]{1,0:T(8,128)(2,1)} %get-tuple-element.8.other_ref), custom_call_target="tpu_custom_call" | custom-call | tf_op jit(solution)/shard_map/basis_rows/pallas_call | solution.py:507
  (1 shorter events, 0.0 us)

commit v4 on v3

--- a/solution.py
+++ b/solution.py
@@ -293,73 +293,93 @@
 
 
 def gram_kernel(
-    owners, total_rows, chunk, own_ref, other_ref, blocks_ref,
-    part_ref, inbox_ref, pair_sems, part_send, part_recv, sum_send, sum_recv, pass_send, pass_recv,
+    owners, total_rows, chunk, own_ref, other_ref, blocks_ref, part_ref, sibling_ref, inbox_ref,
+    pair_sems, half_sems, near_sems, far_sems, part_sems, sum_sems, pass_sems,
 ):
     me = lax.axis_index("blk")
     col = lax.axis_index("col")
+    chips = owners // 2
+    chip = me // 2
+    core = lax.rem(me, 2)
     partner = {"blk": me, "col": 1 - col}
+    sibling = {"blk": 2 * chip + 1 - core, "col": col}
     width = own_ref.shape[1]
     edge = blocks_ref.shape[2]
     half = width // edge
-    own_depth = edge * half * (half + 1) // 2
-    depth = edge * (half * (half + 1) // 2 + half * half // 2)
-    reducers = (depth + chunk - 1) // chunk
-    early = own_depth // chunk
-
-    barrier = pltpu.get_barrier_semaphore()
-
-    def greet(d, carry):
-        pl.semaphore_signal(
-            barrier, inc=1, device_id={"blk": lax.rem(me + d, owners), "col": col},
-            device_id_type=pl.DeviceIdType.MESH,
-        )
-        return carry
-
-    lax.fori_loop(1, owners, greet, 0)
-    pl.semaphore_signal(barrier, inc=1, device_id=partner, device_id_type=pl.DeviceIdType.MESH)
-    pl.semaphore_wait(barrier, owners)
-
-    def rows_of(q):
-        return pl.ds(pl.multiple_of(q * chunk, chunk), chunk)
-
-    def remote(src, dst, send_sem, recv_sem, device):
+    span = sibling_ref.shape[0]
+    reducers = span // chunk
+    base = core * span
+
+    def peer(q):
+        return {"blk": 2 * q + core, "col": col}
+
+    def remote(src, dst, sems, device):
         return pltpu.make_async_remote_copy(
-            src_ref=src, dst_ref=dst, send_sem=send_sem, recv_sem=recv_sem,
+            src_ref=src, dst_ref=dst, send_sem=sems[0], recv_sem=sems[1],
             device_id=device, device_id_type=pl.DeviceIdType.MESH,
         )
 
-    def peer(q):
-        return {"blk": q, "col": col}
+    def rows_at(start, count):
+        return pl.ds(pl.multiple_of(start, 8), count)
+
+    def rows_of(q):
+        return rows_at(base + q * chunk, chunk)
 
     def part_copy(src, q):
         return remote(
-            part_ref.at[rows_of(q)], inbox_ref.at[src], part_send.at[q], part_recv.at[src], peer(q)
+            part_ref.at[rows_of(q)], inbox_ref.at[src],
+            (part_sems.at[0, q], part_sems.at[1, src]), peer(q),
         )
 
     def sum_copy(src, q):
         rows = blocks_ref.at[col, rows_of(src)]
-        return remote(rows, rows, sum_send.at[q], sum_recv.at[src], peer(q))
+        return remote(rows, rows, (sum_sems.at[0, q], sum_sems.at[1, src]), peer(q))
 
     def pass_copy(holder, q):
         rows = blocks_ref.at[holder, rows_of(q)]
-        return remote(rows, rows, pass_send.at[q], pass_recv.at[q], partner)
-
-    def each_peer(step, low, high):
+        return remote(rows, rows, (pass_sems.at[0, q], pass_sems.at[1, q]), partner)
+
+    def share_copy(holder, side, sems):
+        rows = blocks_ref.at[holder, rows_at(side * span, span)]
+        return remote(rows, rows, (sems.at[0], sems.at[1]), sibling)
+
+    def each(step, first=1):
         def turn(d, carry):
-            q = lax.rem(me + d, owners)
-
-            @pl.when((q >= low) & (q < high))
+            step(d)
+            return carry
+
+        lax.fori_loop(first, chips, turn, 0)
+
+    def ahead(d):
+        return lax.rem(chip + d, chips)
+
+    def behind(d):
+        return lax.rem(chip + chips - d, chips)
+
+    def each_reducer(step):
+        def turn(d):
+            q = ahead(d)
+
+            @pl.when(q < reducers)
             def _():
                 step(q)
 
-            return carry
-
-        lax.fori_loop(1, owners, turn, 0)
-
-    pair = remote(own_ref, other_ref, pair_sems.at[0], pair_sems.at[1], partner)
+        each(turn)
+
+    barrier = pltpu.get_barrier_semaphore()
+
+    def greet(device):
+        pl.semaphore_signal(
+            barrier, inc=1, device_id=device, device_id_type=pl.DeviceIdType.MESH
+        )
+
+    greet(partner)
+    greet(sibling)
+    each(lambda d: greet(peer(ahead(d))))
+    pl.semaphore_wait(barrier, chips + 1)
+
+    pair = remote(own_ref, other_ref, (pair_sems.at[0], pair_sems.at[1]), partner)
     pair.start()
-
     own = own_ref[...]
     own_gram = lax.dot_general(
         own, own, (((0,), (0,)), ((), ())), preferred_element_type=jnp.float32
@@ -371,14 +391,18 @@
                 block_row * edge : (block_row + 1) * edge, block_col * edge : (block_col + 1) * edge
             ]
             index += 1
-    each_peer(lambda q: part_copy(me, q).start(), 0, early)
+
+    halves = remote(
+        part_ref.at[rows_at((1 - core) * span, span)], sibling_ref,
+        (half_sems.at[0], half_sems.at[1]), sibling,
+    )
 
     pair.wait()
     other = other_ref[...]
     low_half = jnp.where(col == 0, own, other)
     high_half = jnp.where(col == 0, other, own)
-    span = width // 2
-    low_part = jnp.where(col == 0, low_half[:, :span], low_half[:, span:])
+    side = width // 2
+    low_part = jnp.where(col == 0, low_half[:, :side], low_half[:, side:])
     cross = lax.dot_general(
         high_half, low_part, (((0,), (0,)), ((), ())), preferred_element_type=jnp.float32
     )
@@ -388,48 +412,56 @@
                 block_row * edge : (block_row + 1) * edge, block_col * edge : (block_col + 1) * edge
             ]
             index += 1
-    each_peer(lambda q: part_copy(me, q).start(), early, reducers)
-
-    @pl.when(me < reducers)
+    halves.start()
+    halves.wait()
+    mine = rows_at(base, span)
+    part_ref[mine] += sibling_ref[...]
+    each_reducer(lambda q: part_copy(chip, q).start())
+
+    @pl.when(chip < reducers)
     def _():
         def add(d, total):
-            src = lax.rem(me + owners - d, owners)
-            part_copy(src, me).wait_recv()
+            src = behind(d)
+            part_copy(src, chip).wait_recv()
             return total + inbox_ref[src]
 
-        total = lax.fori_loop(1, owners, add, part_ref[rows_of(me)])
-        blocks_ref[col, rows_of(me)] = total / total_rows
-
-        def send(d, carry):
-            sum_copy(me, lax.rem(me + d, owners)).start()
-            return carry
-
-        lax.fori_loop(1, owners, send, 0)
-        pass_copy(col, me).start()
-
-    def hand_on(d, carry):
-        src = lax.rem(me + owners - d, owners)
+        total = lax.fori_loop(1, chips, add, part_ref[rows_of(chip)])
+        blocks_ref[col, rows_of(chip)] = total / total_rows
+        each(lambda d: sum_copy(chip, ahead(d)).start())
+        pass_copy(col, chip).start()
+
+    def hand_on(d):
+        src = behind(d)
 
         @pl.when(src < reducers)
         def _():
             sum_copy(src, src).wait_recv()
             pass_copy(col, src).start()
 
+    each(hand_on)
+    near = share_copy(col, core, near_sems)
+    near.start()
+
+    def arrive(q, carry):
+        pass_copy(1 - col, q).wait_recv()
         return carry
 
-    lax.fori_loop(1, owners, hand_on, 0)
-
-    def finish(q, carry):
-        pass_copy(1 - col, q).wait_recv()
+    lax.fori_loop(0, reducers, arrive, 0)
+    far = share_copy(1 - col, core, far_sems)
+    far.start()
+    near.wait()
+    far.wait()
+
+    def leave(q, carry):
         pass_copy(col, q).wait_send()
         return carry
 
-    lax.fori_loop(0, reducers, finish, 0)
-    each_peer(lambda q: part_copy(me, q).wait_send(), 0, reducers)
-
-    @pl.when(me < reducers)
+    lax.fori_loop(0, reducers, leave, 0)
+    each_reducer(lambda q: part_copy(chip, q).wait_send())
+
+    @pl.when(chip < reducers)
     def _():
-        each_peer(lambda q: sum_copy(me, q).wait_send(), 0, owners)
+        each(lambda d: sum_copy(chip, ahead(d)).wait_send())
 
 
 def local(tiles, tile_rows, tile_cols, tile_count, sketch, variant_scale):
@@ -483,22 +515,24 @@
     total_rows = own_rows * edge * owners
     half = width // edge
     depth = edge * (half * (half + 1) // 2 + half * half // 2)
-    chunk = -(-depth // (8 * owners)) * 8
-    reducers = -(-depth // chunk)
+    chips = owners // 2
+    chunk = -(-depth // (16 * chips)) * 8
+    span = -(-depth // (2 * chunk)) * chunk
     other_rows, blocks = pl.pallas_call(
         functools.partial(gram_kernel, owners, total_rows, chunk),
         out_shape=(
             jax.ShapeDtypeStruct(power_rows.shape, jnp.bfloat16),
-            jax.ShapeDtypeStruct((2, reducers * chunk, edge), jnp.float32),
+            jax.ShapeDtypeStruct((2, 2 * span, edge), jnp.float32),
         ),
         in_specs=[VMEM_SPEC],
         out_specs=(VMEM_SPEC, VMEM_SPEC),
         scratch_shapes=[
-            pltpu.VMEM((reducers * chunk, edge), jnp.float32),
-            pltpu.VMEM((owners, chunk, edge), jnp.float32),
-            pltpu.SemaphoreType.DMA((2,)),
+            pltpu.VMEM((2 * span, edge), jnp.float32),
+            pltpu.VMEM((span, edge), jnp.float32),
+            pltpu.VMEM((chips, chunk, edge), jnp.float32),
         ]
-        + [pltpu.SemaphoreType.DMA((owners,))] * 6,
+        + [pltpu.SemaphoreType.DMA((2,))] * 4
+        + [pltpu.SemaphoreType.DMA((2, chips))] * 3,
         compiler_params=pltpu.CompilerParams(
             vmem_limit_bytes=VMEM_BYTES, collective_id=0, has_side_effects=True
         ),

time: 154 us -> 146 us (0.948)
  Pallas kernels: 150 us -> 141 us
    pallas_call x1, Pallas kernels: 49.4 us -> 40.7 us  [local(): pl.pallas_call(functools.partial(gram_kernel, owners, total_rows, chunk),...]
where the time goes in v4:
time: 146 us; the launch traced here: 145 us
  Pallas kernels  141 us (97%)
  other arithmetic  2.75 us (2%)
    pallas_call x1, Pallas kernels, local(): pl.pallas_call(functools.partial(exchange_kernel, owners), out_shape=jax....  78.6 us
    pallas_call x1, Pallas kernels, local(): pl.pallas_call(functools.partial(gram_kernel, owners, total_rows, chunk),...  40.7 us
    pallas_call x1, Pallas kernels, local(): pl.pallas_call(basis_kernel, out_shape=jax.ShapeDtypeStruct((own_rows * e...  21.9 us

profile of v4, /device:TPU:0, one launch (start us, length us, event | category | flops | bytes accessed | tf_op | source)
XLA Modules:
  0.0 145.3 jit_solution(1337635933635149633)
XLA Ops:
  0.7 0.7 multiply_add_fusion
  1.4 0.6 select_reduce_fusion.slot_ref
  2.0 0.1 select_reduce_fusion.1
  2.1 0.7 broadcast_in_dim.42.wanted_ref
  2.8 1.3 reshape.25
  4.1 78.6 %exchange_rows.1.own_ref = bf16[512,256]{1,0:T(8,128)(2,1)} custom-call(s32[64]{0:T(128)} %select_reduce_fusion.slot_ref, s32[16,1,128]{2,1,0:T(1,128)} %broadcast_in_dim.42.wanted_ref, f32[32,1,128]{2,1,0:T(1,128)} %bitcast.6, bf16[24,128,128]{2,1,0:T(8,128)(2,1)} %tiles_ref.1, bf16[32,128,256]{2,1,0:T(8,128)(2,1)} %bitcast.5), custom_call_target="tpu_custom_call" | custom-call | tf_op jit(solution)/shard_map/exchange_rows/pallas_call | solution.py:484
  82.7 40.7 %gram_blocks.1 = (bf16[512,256]{1,0:T(8,128)(2,1)}, f32[2,640,128]{2,1,0:T(8,128)}) custom-call(bf16[512,256]{1,0:T(8,128)(2,1)} %exchange_rows.1.own_ref), custom_call_target="tpu_custom_call" | custom-call | tf_op jit(solution)/shard_map/gram_blocks/pallas_call | solution.py:521
  123.4 21.9 %basis_rows.1 = f32[512,256]{1,0:T(8,128)} custom-call(s32[1]{0:T(128)} %bitcast.col_ref, f32[2,640,128]{2,1,0:T(8,128)} %get-tuple-element.7.blocks_ref, bf16[512,256]{1,0:T(8,128)(2,1)} %exchange_rows.1.own_ref, bf16[512,256]{1,0:T(8,128)(2,1)} %get-tuple-element.8.other_ref), custom_call_target="tpu_custom_call" | custom-call | tf_op jit(solution)/shard_map/basis_rows/pallas_call | solution.py:541
  (1 shorter events, 0.0 us)

commit v5 on v4

--- a/solution.py
+++ b/solution.py
@@ -37,11 +37,21 @@
 
         lax.fori_loop(first, owners, turn, 0)
 
+    span = owners // 2
+    side = lax.div(me, span)
+    place = lax.rem(me, span)
+
+    def turn_of(d):
+        near = lax.div(d - 1, span)
+        return lax.rem(side + 1 - near, 2) * span, d - 1 - near * (span - 1)
+
     def ahead(d):
-        return lax.rem(me + d, owners)
+        first, step = turn_of(d)
+        return first + lax.rem(place + step, span)
 
     def behind(d):
-        return lax.rem(me + owners - d, owners)
+        first, step = turn_of(d)
+        return first + lax.rem(place + span - step, span)
 
     def greet(d):
         pl.semaphore_signal(

time: 146 us -> 145 us (level)
    pallas_call x1, Pallas kernels: 40.7 us -> 29.3 us  [local(): pl.pallas_call(functools.partial(gram_kernel, owners, total_rows, chunk),...]
    pallas_call x1, Pallas kernels: 78.6 us -> 89.3 us  [local(): pl.pallas_call(functools.partial(exchange_kernel, owners), out_shape=jax....]
where the time goes in v5:
time: 145 us
  Pallas kernels  141 us (97%)
  other arithmetic  2.75 us (2%)
    pallas_call x1, Pallas kernels, local(): pl.pallas_call(functools.partial(exchange_kernel, owners), out_shape=jax....  89.3 us
    pallas_call x1, Pallas kernels, local(): pl.pallas_call(functools.partial(gram_kernel, owners, total_rows, chunk),...  29.3 us
    pallas_call x1, Pallas kernels, local(): pl.pallas_call(basis_kernel, out_shape=jax.ShapeDtypeStruct((own_rows * e...  21.9 us

profile of v5, /device:TPU:0, one launch (start us, length us, event | category | flops | bytes accessed | tf_op | source)
XLA Modules:
  0.0 144.6 jit_solution(16652444517369767325)
XLA Ops:
  0.7 0.7 multiply_add_fusion
  1.4 0.6 select_reduce_fusion.slot_ref
  2.0 0.1 select_reduce_fusion.1
  2.1 0.7 broadcast_in_dim.42.wanted_ref
  2.8 1.3 reshape.25
  4.1 89.3 %exchange_rows.1.own_ref = bf16[512,256]{1,0:T(8,128)(2,1)} custom-call(s32[64]{0:T(128)} %select_reduce_fusion.slot_ref, s32[16,1,128]{2,1,0:T(1,128)} %broadcast_in_dim.42.wanted_ref, f32[32,1,128]{2,1,0:T(1,128)} %bitcast.6, bf16[24,128,128]{2,1,0:T(8,128)(2,1)} %tiles_ref.1, bf16[32,128,256]{2,1,0:T(8,128)(2,1)} %bitcast.5), custom_call_target="tpu_custom_call" | custom-call | tf_op jit(solution)/shard_map/exchange_rows/pallas_call | solution.py:494
  93.4 29.3 %gram_blocks.1 = (bf16[512,256]{1,0:T(8,128)(2,1)}, f32[2,640,128]{2,1,0:T(8,128)}) custom-call(bf16[512,256]{1,0:T(8,128)(2,1)} %exchange_rows.1.own_ref), custom_call_target="tpu_custom_call" | custom-call | tf_op jit(solution)/shard_map/gram_blocks/pallas_call | solution.py:531
  122.8 21.9 %basis_rows.1 = f32[512,256]{1,0:T(8,128)} custom-call(s32[1]{0:T(128)} %bitcast.col_ref, f32[2,640,128]{2,1,0:T(8,128)} %get-tuple-element.7.blocks_ref, bf16[512,256]{1,0:T(8,128)(2,1)} %exchange_rows.1.own_ref, bf16[512,256]{1,0:T(8,128)(2,1)} %get-tuple-element.8.other_ref), custom_call_target="tpu_custom_call" | custom-call | tf_op jit(solution)/shard_map/basis_rows/pallas_call | solution.py:551
  (1 shorter events, 0.0 us)

commit v6 on v5

--- a/solution.py
+++ b/solution.py
@@ -207,7 +207,7 @@
         for i in range(PANEL):
             pivot = jnp.broadcast_to(columns[i][0][i : i + 1, :], (PANEL, edge))
             pivots = jnp.where(sublanes == i, pivot, pivots)
-            factor = 1.0 / pivot
+            factor = pl.reciprocal(pivot)
             row = jnp.broadcast_to(live[0][i : i + 1, :], (PANEL, edge))
             heads = [
                 jnp.broadcast_to(columns[k][0][i : i + 1, :], (PANEL, edge))

time: 145 us -> 145 us (level)
  no operation moved by 1% of the time
where the time goes in v6:
time: 145 us
  Pallas kernels  141 us (97%)
  other arithmetic  2.75 us (2%)
    pallas_call x1, Pallas kernels, local(): pl.pallas_call(functools.partial(exchange_kernel, owners), out_shape=jax....  89.3 us
    pallas_call x1, Pallas kernels, local(): pl.pallas_call(functools.partial(gram_kernel, owners, total_rows, chunk),...  29.3 us
    pallas_call x1, Pallas kernels, local(): pl.pallas_call(basis_kernel, out_shape=jax.ShapeDtypeStruct((own_rows * e...  21.9 us

profile of v6, /device:TPU:0, one launch (start us, length us, event | category | flops | bytes accessed | tf_op | source)
XLA Modules:
  0.0 144.6 jit_solution(16652444517369767325)
XLA Ops:
  0.7 0.7 multiply_add_fusion
  1.4 0.6 select_reduce_fusion.slot_ref
  2.0 0.1 select_reduce_fusion.1
  2.1 0.7 broadcast_in_dim.42.wanted_ref
  2.8 1.3 reshape.25
  4.1 89.3 %exchange_rows.1.own_ref = bf16[512,256]{1,0:T(8,128)(2,1)} custom-call(s32[64]{0:T(128)} %select_reduce_fusion.slot_ref, s32[16,1,128]{2,1,0:T(1,128)} %broadcast_in_dim.42.wanted_ref, f32[32,1,128]{2,1,0:T(1,128)} %bitcast.6, bf16[24,128,128]{2,1,0:T(8,128)(2,1)} %tiles_ref.1, bf16[32,128,256]{2,1,0:T(8,128)(2,1)} %bitcast.5), custom_call_target="tpu_custom_call" | custom-call | tf_op jit(solution)/shard_map/exchange_rows/pallas_call | solution.py:494
  93.4 29.3 %gram_blocks.1 = (bf16[512,256]{1,0:T(8,128)(2,1)}, f32[2,640,128]{2,1,0:T(8,128)}) custom-call(bf16[512,256]{1,0:T(8,128)(2,1)} %exchange_rows.1.own_ref), custom_call_target="tpu_custom_call" | custom-call | tf_op jit(solution)/shard_map/gram_blocks/pallas_call | solution.py:531
  122.8 21.9 %basis_rows.1 = f32[512,256]{1,0:T(8,128)} custom-call(s32[1]{0:T(128)} %bitcast.col_ref, f32[2,640,128]{2,1,0:T(8,128)} %get-tuple-element.7.blocks_ref, bf16[512,256]{1,0:T(8,128)(2,1)} %exchange_rows.1.own_ref, bf16[512,256]{1,0:T(8,128)(2,1)} %get-tuple-element.8.other_ref), custom_call_target="tpu_custom_call" | custom-call | tf_op jit(solution)/shard_map/basis_rows/pallas_call | solution.py:551
  (1 shorter events, 0.0 us)
